TPU v7x, 512 devices: a whole 4x4x16 slice. The times are simulated.
512 devices in a mesh: pipe: 8 (over x, core), dp: 64 (over y, z).
Axes of the slice: x: 4, y: 4, z: 16, core: 2. Of those that a mesh axis runs over, the one named last changes fastest.
Arguments:
- acts: bfloat16 [8, 8192, 8192], P('pipe', 'dp'), may hold values from -6 to 6
- incoming: bfloat16 [8, 8192, 8192], P('pipe', 'dp'), may hold values from -6 to 6
- proj_in: bfloat16 [64, 8192], P(None, 'dp'), may hold values from -0.0625 to 0.0625
- proj_out: bfloat16 [64, 8192], P(None, 'dp'), may hold values from -0.0625 to 0.0625
- valid_rows: bfloat16 [8, 128, 4096], P('pipe', 'dp'), may hold values from -0.09375 to 0.09375
- lengths: int32 [64], P('dp'), may hold values from 1 to 128, 7168 in all
- domains: int32 [64], replicated, may hold values from 0 to 63
Outputs:
- domain_gram: float32 [8, 64, 128, 128], P('pipe', 'dp')
All inputs are finite; a program needn't handle non-finite values. No bound on the sum of `lengths` on one device may be relied on, other than what follows from the above.
Results may differ from a plain program's by a relative error of at most 0.004.
Values may be sent and summed in bfloat16 or wider, within the bound.
No kernel may reach another device: no remote copies, remote signals or barrier semaphores. Data moves between devices by JAX's collectives and lax.ppermute only.
A program may use at most 128 MiB of HBM per device.

v0:
```python
import jax
import jax.numpy as jnp
from jax import lax
from jax.sharding import PartitionSpec as P

highest_precision = lax.Precision.HIGHEST


def entering(value, axis, combine, identity):
    length, place = (lax.axis_size(axis), lax.axis_index(axis))
    everything = lax.all_gather(value.astype(jnp.bfloat16), axis)
    start = jnp.broadcast_to(jnp.asarray(identity, value.dtype), value.shape)

    def lap(k, before):
        at = length - 1 - k
        reached = at > place
        new = combine(before, everything[at].astype(value.dtype))
        return jnp.where(reached, new, before)

    return lax.fori_loop(0, length, lap, start)


def add_terms(earlier, later):
    return earlier + later


def body(acts, incoming, proj_in, proj_out, valid_rows, lengths, domains):
    layer_act = acts[0]
    branch = incoming[0]
    rows_here = layer_act.shape[0]
    proj_size = proj_in.shape[0]
    grad_term = branch.astype(jnp.float32)
    above = entering(grad_term, "pipe", add_terms, jnp.zeros_like(grad_term))
    source = above + grad_term
    empty = jnp.zeros((rows_here, proj_size), jnp.float32)
    pieces = (
        lax.all_gather(proj_in, "dp", axis=1, tiled=True),
        lax.all_gather(proj_out, "dp", axis=1, tiled=True),
    )
    new_act = lax.dot_general(
        layer_act, pieces[0], (((1,), (1,)), ((), ())), preferred_element_type=jnp.float32
    )
    if source.dtype == jnp.float32:
        new_grad = (empty, empty)[1] + lax.dot_general(
            source,
            pieces[1].astype(jnp.float32),
            (((1,), (1,)), ((), ())),
            precision=highest_precision,
        )
    else:
        new_grad = lax.dot_general(
            source, pieces[1], (((1,), (1,)), ((), ())), preferred_element_type=jnp.float32
        )
    live_count = lengths[0]
    positions = lax.iota(jnp.int32, rows_here)
    weights = jnp.where(positions < live_count, 1.0, 0.0).astype(jnp.float32) / live_count.astype(
        jnp.float32
    )
    scaled = new_grad * weights[:, None]
    grad_row = lax.dot_general(
        scaled, new_act, (((0,), (0,)), ((), ())), precision=highest_precision
    )
    grad_row = grad_row.reshape(1, proj_size * proj_size).astype(jnp.bfloat16)
    valid_full = lax.all_gather(valid_rows, "dp", axis=1, tiled=True)[0]
    my_index = lax.axis_index("dp")
    scores = lax.dot_general(
        lax.all_gather(grad_row, "dp", axis=0, tiled=True),
        valid_full,
        (((1,), (1,)), ((), ())),
        preferred_element_type=jnp.float32,
    )
    owned = domains == my_index
    kept = scores * owned.astype(jnp.float32)[:, None]
    gram = lax.dot_general(kept, scores, (((0,), (0,)), ((), ())), precision=highest_precision)
    return gram[None, None]


def solution(mesh):
    placed = (
        P("pipe", "dp", None),
        P("pipe", "dp", None),
        P(None, "dp"),
        P(None, "dp"),
        P("pipe", "dp", None),
        P("dp"),
        P(),
    )
    return jax.shard_map(
        body, mesh=mesh, in_specs=placed, out_specs=P("pipe", "dp", None, None), check_vma=False
    )
```

profile of v0, /device:TPU:4, one launch (start us, length us, event | category | flops | bytes accessed | tf_op | source)
XLA Modules:
  0.0 522.5 jit_solution(17948236121018723122)
XLA Ops:
  6.5 0.0 copy-start
  6.5 0.0 all-gather.10.cloned.1.call-start
  6.5 0.7 all-gather.10.cloned.1.call-update
  7.3 0.0 all-gather.6.cloned.1.call-start
  7.3 0.7 all-gather.6.cloned.1.call-update
  8.0 0.0 all-gather.8.cloned.1.call-start
  8.1 0.7 all-gather.8.cloned.1.call-update
  8.7 0.0 all-gather.12.cloned.1.call-start
  8.8 1.4 copy.10
  10.1 0.0 all-gather.12.cloned.1.call-update
  10.9 0.7 compare_convert_fusion
  11.5 134.6 %all-gather.10.cloned.1.call-done = bf16[64,8192]{1,0:T(8,128)(2,1)} async-done(((bf16[64,128]{1,0:T(8,128)(2,1)}), bf16[64,8192]{1,0:T(8,128)(2,1)}) %all-gather.10.cloned.1.call-update) | async-done | bytes 1048592 | tf_op jit(solution)/shard_map/all_gather | solution.py:37
  146.1 0.0 copy-done
  146.1 2.1 fusion.2
  148.2 88.0 %all-gather.6.cloned.1.call-done = bf16[8,128,8192]{2,1,0:T(8,128)(2,1)} async-done(((bf16[1,128,8192]{2,1,0:T(8,128)(2,1)}), bf16[8,128,8192]{2,1,0:T(8,128)(2,1)}) %all-gather.6.cloned.1.call-update) | async-done | bytes 16777232 | tf_op jit(solution)/shard_map/all_gather | solution.py:11
  236.1 41.8 %while.16 = (s32[]{:T(128)}, f32[128,8192]{1,0:T(8,128)}, s32[]{:T(128)}, bf16[8,128,8192]{2,1,0:T(8,128)(2,1)}, s32[]{:T(128)}, /*index=5*/s32[]{:T(128)}, s32[]{:T(128)}, s32[]{:T(128)}) while((s32[]{:T(128)}, f32[128,8192]{1,0:T(8,128)}, s32[]{:T(128)}, bf16[8,128,8192]{2,1,0:T(8,128)(2,1)}, s32[]{:T(128)}, ...), condition=%wide.region_1.2_spmd.clone, body=%wide.region_0.1_spmd.clone.sunk | while | flops 4194312 | bytes 10485915 | solution.py:20
  236.1 4.1 add_select_fusion.2
  240.2 5.4 %add_select_fusion.2 = f32[128,8192]{1,0:T(8,128)} fusion(f32[128,8192]{1,0:T(8,128)} %get-tuple-element.173, bf16[8,128,8192]{2,1,0:T(8,128)(2,1)} %get-tuple-element.183, s32[]{:T(128)S(6)} %select_n.54, pred[]{:T(512)S(6)} %compare.3, pred[]{:T(512)S(6)} %gt.12), kind=kLoop, calls=%fused_computation.clone.1 | loop fusion | flops 4194304 | bytes 10485766 | tf_op jit(solution)/shard_map/while/body/eval_jaxpr/jit(_where)/select_n | solution.py:18
  245.6 5.4 %add_select_fusion.2 = f32[128,8192]{1,0:T(8,128)} fusion(f32[128,8192]{1,0:T(8,128)} %get-tuple-element.173, bf16[8,128,8192]{2,1,0:T(8,128)(2,1)} %get-tuple-element.183, s32[]{:T(128)S(6)} %select_n.54, pred[]{:T(512)S(6)} %compare.3, pred[]{:T(512)S(6)} %gt.12), kind=kLoop, calls=%fused_computation.clone.1 | loop fusion | flops 4194304 | bytes 10485766 | tf_op jit(solution)/shard_map/while/body/eval_jaxpr/jit(_where)/select_n | solution.py:18
  251.0 5.4 %add_select_fusion.2 = f32[128,8192]{1,0:T(8,128)} fusion(f32[128,8192]{1,0:T(8,128)} %get-tuple-element.173, bf16[8,128,8192]{2,1,0:T(8,128)(2,1)} %get-tuple-element.183, s32[]{:T(128)S(6)} %select_n.54, pred[]{:T(512)S(6)} %compare.3, pred[]{:T(512)S(6)} %gt.12), kind=kLoop, calls=%fused_computation.clone.1 | loop fusion | flops 4194304 | bytes 10485766 | tf_op jit(solution)/shard_map/while/body/eval_jaxpr/jit(_where)/select_n | solution.py:18
  256.4 5.4 %add_select_fusion.2 = f32[128,8192]{1,0:T(8,128)} fusion(f32[128,8192]{1,0:T(8,128)} %get-tuple-element.173, bf16[8,128,8192]{2,1,0:T(8,128)(2,1)} %get-tuple-element.183, s32[]{:T(128)S(6)} %select_n.54, pred[]{:T(512)S(6)} %compare.3, pred[]{:T(512)S(6)} %gt.12), kind=kLoop, calls=%fused_computation.clone.1 | loop fusion | flops 4194304 | bytes 10485766 | tf_op jit(solution)/shard_map/while/body/eval_jaxpr/jit(_where)/select_n | solution.py:18
  261.8 5.4 %add_select_fusion.2 = f32[128,8192]{1,0:T(8,128)} fusion(f32[128,8192]{1,0:T(8,128)} %get-tuple-element.173, bf16[8,128,8192]{2,1,0:T(8,128)(2,1)} %get-tuple-element.183, s32[]{:T(128)S(6)} %select_n.54, pred[]{:T(512)S(6)} %compare.3, pred[]{:T(512)S(6)} %gt.12), kind=kLoop, calls=%fused_computation.clone.1 | loop fusion | flops 4194304 | bytes 10485766 | tf_op jit(solution)/shard_map/while/body/eval_jaxpr/jit(_where)/select_n | solution.py:18
  267.1 5.4 %add_select_fusion.2 = f32[128,8192]{1,0:T(8,128)} fusion(f32[128,8192]{1,0:T(8,128)} %get-tuple-element.173, bf16[8,128,8192]{2,1,0:T(8,128)(2,1)} %get-tuple-element.183, s32[]{:T(128)S(6)} %select_n.54, pred[]{:T(512)S(6)} %compare.3, pred[]{:T(512)S(6)} %gt.12), kind=kLoop, calls=%fused_computation.clone.1 | loop fusion | flops 4194304 | bytes 10485766 | tf_op jit(solution)/shard_map/while/body/eval_jaxpr/jit(_where)/select_n | solution.py:18
  272.5 5.4 %add_select_fusion.2 = f32[128,8192]{1,0:T(8,128)} fusion(f32[128,8192]{1,0:T(8,128)} %get-tuple-element.173, bf16[8,128,8192]{2,1,0:T(8,128)(2,1)} %get-tuple-element.183, s32[]{:T(128)S(6)} %select_n.54, pred[]{:T(512)S(6)} %compare.3, pred[]{:T(512)S(6)} %gt.12), kind=kLoop, calls=%fused_computation.clone.1 | loop fusion | flops 4194304 | bytes 10485766 | tf_op jit(solution)/shard_map/while/body/eval_jaxpr/jit(_where)/select_n | solution.py:18
  277.9 93.9 %all-gather.8.cloned.1.call-done = bf16[64,8192]{1,0:T(8,128)(2,1)} async-done(((bf16[64,128]{1,0:T(8,128)(2,1)}), bf16[64,8192]{1,0:T(8,128)(2,1)}) %all-gather.8.cloned.1.call-update) | async-done | bytes 1048592 | tf_op jit(solution)/shard_map/all_gather | solution.py:38
  371.8 5.8 %fusion.4 = f32[128,64]{0,1:T(8,128)S(1)} fusion(bf16[64,8192]{1,0:T(8,128)(2,1)} %all-gather.8.cloned.1.call-done, f32[128,8192]{1,0:T(8,128)} %get-tuple-element.115, bf16[1,128,8192]{2,1,0:T(8,128)(2,1)} %param.10, f32[128]{0:T(128)S(1)} %fusion.12), kind=kOutput, calls=%fused_computation.7 | convolution fusion | flops 807411712 | bytes 7373312 | tf_op jit(solution)/shard_map/dot_general | solution.py:44
  377.6 0.2 convolution_convert_fusion
  377.8 0.1 reshape.28
  377.9 100.0 %all-gather = bf16[64,1,4096]{2,1,0:T(2,128)(2,1)S(1)} all-gather(bf16[1,1,4096]{2,1,0:T(2,128)(2,1)S(1)} %reshape.28), channel_id=1, replica_groups=mesh['pipe'=8,'dp'=64] {'dp'}, dimensions={0}, use_global_device_ids=true | all-gather | bytes 532480 | tf_op jit(solution)/shard_map/all_gather | solution.py:67
  477.8 33.8 %all-gather.12.cloned.1.call-done = bf16[1,128,4096]{2,0,1:T(2,128)(2,1)} async-done(((bf16[1,2,4096]{2,0,1:T(2,128)(2,1)}), bf16[1,128,4096]{2,0,1:T(2,128)(2,1)}) %all-gather.12.cloned.1.call-update) | async-done | bytes 1048592 | tf_op jit(solution)/shard_map/all_gather | solution.py:64
  511.7 3.3 fusion.5
  515.0 1.0 convolution_bitcast_fusion
  (2 shorter events, 0.0 us)
Async XLA Ops:
  6.5 139.6 %copy-start = (bf16[1,128,8192]{2,1,0:T(8,128)(2,1)S(1)}, bf16[1,128,8192]{2,1,0:T(8,128)(2,1)}, u32[]{:S(2)}) copy-start(bf16[1,128,8192]{2,1,0:T(8,128)(2,1)} %param.9) | copy-start | bytes 6291460
  6.5 139.6 %all-gather.10.cloned.1.call-start = ((), (), s32[]{:S(2)}) async-start(), calls=%async_computation.2 | async-start | bytes 1064960 | tf_op jit(solution)/shard_map/all_gather | solution.py:37
  7.3 228.9 %all-gather.6.cloned.1.call-start = ((), (), s32[]{:S(2)}) async-start(), calls=%async_computation | async-start | bytes 18874368 | tf_op jit(solution)/shard_map/all_gather | solution.py:11
  8.0 363.8 %all-gather.8.cloned.1.call-start = ((), (), s32[]{:S(2)}) async-start(), calls=%async_computation.1 | async-start | bytes 1064960 | tf_op jit(solution)/shard_map/all_gather | solution.py:38
  8.7 502.9 %all-gather.12.cloned.1.call-start = ((), (), s32[]{:S(2)}) async-start(), calls=%async_computation.3 | async-start | bytes 2129920 | tf_op jit(solution)/shard_map/all_gather | solution.py:64
Sparse Core Ops, SparseCore 0:
  10.3 135.7 all-gather.9
  148.3 87.8 all-gather.5
  239.1 132.7 all-gather.7
  374.6 137.0 all-gather.11
where the time goes:
time: 523 us
  waiting for transfers between devices  352 us (67%)
  blocking collectives  100 us (19%)
  other arithmetic  42.4 us (8%)
  between operations  13.8 us (3%)
  matrix products  12.3 us (2%)
    all_gather x1, waiting for transfers between devices, body(): lax.all_gather(proj_in, 'dp', axis=1, tiled=True)  135 us
    all_gather x1, blocking collectives, body(): lax.all_gather(grad_row, 'dp', axis=0, tiled=True)  100 us
    all_gather x1, waiting for transfers between devices, body(): lax.all_gather(proj_out, 'dp', axis=1, tiled=True)  93.9 us
    all_gather x1, waiting for transfers between devices, entering(): everything = lax.all_gather(value.astype(jnp.bfloat16), axis)  88 us
    select_n x8, other arithmetic, lap(): return jnp.where(reached, new, before)  41.8 us
    all_gather x1, waiting for transfers between devices, body(): valid_full = lax.all_gather(valid_rows, 'dp', axis=1, tiled=True)[0]  33.8 us
  transfers between devices with their start and end apart: 4, of which 4 were waited for; matrix products, arithmetic and copies ran while one was open for 10% of the time, Pallas kernels for 0%

commit v1 on v0

v1 whole, which is shorter than its diff:
```python
import jax
import jax.numpy as jnp
from jax import lax
from jax.experimental import pallas as pl
from jax.experimental.pallas import tpu as pltpu
from jax.sharding import Mesh
from jax.sharding import PartitionSpec as P

HIGHEST = lax.Precision.HIGHEST
NX, NC, NY, NZ = 4, 2, 4, 16
NT = (((1,), (1,)), ((), ()))
f32, bf16 = jnp.float32, jnp.bfloat16


def spread(block, axes, count):
    sent = jnp.broadcast_to(block[None], (count,) + block.shape)
    return lax.all_to_all(sent, axes, 0, 0)


def project_kernel(w_ref, act_own, act_par, inc_own, inc_par, out_ref, acc_ref):
    step = pl.program_id(0)

    @pl.when(step == 0)
    def _():
        acc_ref[...] = jnp.zeros_like(acc_ref)

    w = jnp.concatenate(
        [w_ref[:, 0, z].reshape(NX * 16, 128) for z in range(NZ)], axis=1
    )
    act = jnp.concatenate([act_own[...], act_par[...]], axis=0)
    inc = jnp.concatenate([inc_own[...], inc_par[...]], axis=0)
    acc_ref[0] += lax.dot_general(w, act, NT, preferred_element_type=f32)
    acc_ref[1] += lax.dot_general(w, inc, NT, preferred_element_type=f32)

    @pl.when(step == NY - 1)
    def _():
        my_x, my_c = lax.axis_index("x"), lax.axis_index("c")
        own_a, par_a = acc_ref[0, :, 0:128], acc_ref[0, :, 128:256]
        own_p, par_p = acc_ref[1, :, 0:128], acc_ref[1, :, 128:256]
        both = own_p + par_p
        odd = jnp.where(my_c == 1, own_p, par_p)
        zero = jnp.zeros_like(both)
        row = lax.broadcasted_iota(jnp.int32, (64, 128), 0)
        is_act = lax.rem(lax.div(row, 8), 2) == 0
        for x in range(NX):
            for c in range(NC):
                here = x == my_x
                upper = jnp.where(x < my_x, both, zero)
                grad = jnp.where(here, both if c == 0 else odd, upper)
                act_c = jnp.where(here, jnp.where(my_c == c, own_a, par_a), zero)
                out_ref[x * NC + c] = jnp.where(is_act, act_c, grad)


def project(w, act_own, act_par, inc_own, inc_par):
    wide = act_own.shape[1] // NY
    data = pl.BlockSpec((128, wide), lambda i: (0, i))
    return pl.pallas_call(
        project_kernel,
        grid=(NY,),
        out_shape=jax.ShapeDtypeStruct((NX * NC, 64, 128), f32),
        in_specs=[pl.BlockSpec((NX, 1, NZ, 16, 128), lambda i: (0, i, 0, 0, 0))] + [data] * 4,
        out_specs=pl.BlockSpec((NX * NC, 64, 128), lambda i: (0, 0, 0)),
        scratch_shapes=[pltpu.VMEM((2, 64, 256), f32)],
        compiler_params=pltpu.CompilerParams(vmem_limit_bytes=32 * 2**20),
        cost_estimate=pl.CostEstimate(
            flops=2 * 256 * 8192 * 64 * 2, bytes_accessed=9 * 2**20, transcendentals=0
        ),
    )(w, act_own, act_par, inc_own, inc_par)


def score_kernel(len_ref, parts_ref, valid_ref, out_ref):
    live = len_ref[0]
    tok = lax.broadcasted_iota(jnp.int32, (32, 128), 1)
    weight = jnp.where(tok < live, 1.0, 0.0).astype(f32) / live.astype(f32)
    totals = []
    for c in range(NC):
        total = parts_ref[c]
        for x in range(1, NX):
            total = total + parts_ref[x * NC + c]
        totals.append(total.reshape(NX, 2, 8, 128))
    act = jnp.concatenate([t[:, 0].reshape(32, 128) for t in totals], axis=0)
    row = jnp.concatenate(
        [
            lax.dot_general(
                t[:, 1].reshape(32, 128) * weight, act, NT,
                precision=HIGHEST, preferred_element_type=f32,
            )
            for t in totals
        ],
        axis=1,
    )
    row = row.astype(bf16).astype(f32)
    part = jnp.sum(valid_ref[...].astype(f32) * row[None], axis=1)
    out_ref[...] = lax.dot_general(
        jnp.ones((64, 128), f32), part, NT, precision=HIGHEST, preferred_element_type=f32
    )


def score(lengths, parts, valid):
    vmem = pl.BlockSpec(memory_space=pltpu.VMEM)
    return pl.pallas_call(
        score_kernel,
        out_shape=jax.ShapeDtypeStruct((64, 128), f32),
        in_specs=[pl.BlockSpec(memory_space=pltpu.SMEM), vmem, vmem],
        out_specs=vmem,
        compiler_params=pltpu.CompilerParams(vmem_limit_bytes=32 * 2**20),
        cost_estimate=pl.CostEstimate(
            flops=2 * 128 * 4096, bytes_accessed=2**20, transcendentals=0
        ),
    )(lengths, parts, valid)


def body(acts, incoming, proj_in, proj_out, valid_rows, lengths, domains):
    x, c = lax.axis_index("x"), lax.axis_index("c")
    y, z = lax.axis_index("y"), lax.axis_index("z")
    swap = [(0, 1), (1, 0)]
    act_own, inc_own = acts[0], incoming[0]
    mine_in = lax.dynamic_slice(proj_in, (c * 32 + x * 8, 0), (8, 128))
    mine_out = lax.dynamic_slice(
        proj_out.reshape(32, 2, 128), (x * 8, c, 0), (8, 1, 128)
    ).reshape(8, 128)
    mine = jnp.concatenate([mine_in, mine_out], axis=0)
    along_z = spread(mine, "z", NZ)
    act_par = lax.ppermute(act_own, "c", swap)
    inc_par = lax.ppermute(inc_own, "c", swap)
    w = spread(along_z, ("x", "y"), NX * NY).reshape(NX, NY, NZ, 16, 128)
    valid = spread(spread(valid_rows.reshape(64, 128), "z", NZ), "y", NY)
    parts = lax.all_to_all(project(w, act_own, act_par, inc_own, inc_par), ("x", "c"), 0, 0)
    scores = score(lengths, parts, valid.reshape(128, 32, 128))
    scores = lax.all_to_all(scores.reshape(64, 1, 128), ("y", "z"), 0, 0).reshape(64, 128)
    owned = (domains == y * NZ + z).astype(f32)
    kept = scores * owned[:, None]
    gram = lax.dot_general(kept, scores, (((0,), (0,)), ((), ())), precision=HIGHEST)
    return gram[None, None]


def solution(mesh):
    fine = Mesh(mesh.devices.reshape(NX, NC, NY, NZ), ("x", "c", "y", "z"))
    pipe, dp = ("x", "c"), ("y", "z")
    placed = (
        P(pipe, dp, None),
        P(pipe, dp, None),
        P(None, dp),
        P(None, dp),
        P(pipe, dp, None),
        P(dp),
        P(),
    )
    return jax.shard_map(
        body, mesh=fine, in_specs=placed, out_specs=P(pipe, dp, None, None), check_vma=False
    )
```

time: 523 us -> 126 us (0.24)
  the two profiles are of different devices: /device:TPU:4 before, /device:TPU:8 now
where the time goes in v1:
time: 126 us; the launch traced here: 125 us
  waiting for transfers between devices  45.8 us (36%)
  starting transfers between devices  43.4 us (34%)
  blocking collectives  18.7 us (15%)
  local copies, waits for them, and re-layouts  8.16 us (6%)
  Pallas kernels  7.16 us (6%)
    all_to_all x3, waiting for transfers between devices, spread(): return lax.all_to_all(sent, axes, 0, 0)  25.5 us
    all_to_all x3, starting transfers between devices, spread(): return lax.all_to_all(sent, axes, 0, 0)  23.7 us
    all_to_all x1, blocking collectives, spread(): return lax.all_to_all(sent, axes, 0, 0)  18.7 us
    all_to_all x1, waiting for transfers between devices, body(): lax.all_to_all(scores.reshape(64, 1, 128), ('y', 'z'), 0, 0)  13.4 us
    all_to_all x1, starting transfers between devices, body(): lax.all_to_all(scores.reshape(64, 1, 128), ('y', 'z'), 0, 0)  12 us
    all_to_all x1, waiting for transfers between devices, body(): lax.all_to_all(project(w, act_own, act_par, inc_own, inc_par), ('x', 'c')...  6.8 us
    pallas_call x1, Pallas kernels, project(): pl.pallas_call(project_kernel, grid=(NY,), out_shape=jax.ShapeDtypeStruct...  5.73 us
    unnamed x9, local copies, waits for them, and re-layouts  3.9 us
  transfers between devices with their start and end apart: 7, of which 5 were waited for; matrix products, arithmetic and copies ran while one was open for 2% of the time, Pallas kernels for 5%

profile of v1, /device:TPU:8, one launch (start us, length us, event | category | flops | bytes accessed | tf_op | source)
XLA Modules:
  0.0 125.0 jit_solution(13009720371288705278)
XLA Ops:
  0.0 0.0 copy-start
  0.0 0.7 copy-done
  0.7 0.7 constant_dynamic-slice_fusion.1
  1.4 0.6 broadcast_in_dim.12
  2.1 15.2 %all-to-all-start = ((bf16[16,16,128]{2,1,0:T(8,128)(2,1)}), bf16[16,16,128]{2,1,0:T(8,128)(2,1)S(1)}, u32[]{:S(2)}, u32[]{:S(2)}) async-start(bf16[16,16,128]{2,1,0:T(8,128)(2,1)} %broadcast_in_dim.12), calls=%async_computation | async-start | bytes 131072 | tf_op jit(solution)/shard_map/all_to_all | solution.py:17
  17.3 0.7 broadcast_in_dim.14
  18.0 12.0 %all-to-all-done = bf16[16,16,128]{2,1,0:T(8,128)(2,1)S(1)} async-done(((bf16[16,16,128]{2,1,0:T(8,128)(2,1)}), bf16[16,16,128]{2,1,0:T(8,128)(2,1)S(1)}, u32[]{:S(2)}, u32[]{:S(2)}) %all-to-all-start) | async-done | bytes 65568 | tf_op jit(solution)/shard_map/all_to_all | solution.py:17
  30.0 0.8 broadcast_in_dim.15
  30.8 3.5 %all-to-all-start.3 = ((bf16[16,64,128]{2,1,0:T(8,128)(2,1)}), bf16[16,64,128]{2,1,0:T(8,128)(2,1)S(1)}, u32[]{:S(2)}, u32[]{:S(2)}) async-start(bf16[16,64,128]{2,1,0:T(8,128)(2,1)} %broadcast_in_dim.15), calls=%async_computation.3 | async-start | bytes 524288 | tf_op jit(solution)/shard_map/all_to_all | solution.py:17
  34.3 1.9 %collective-permute-start = (bf16[128,8192]{1,0:T(8,128)(2,1)}, bf16[128,8192]{1,0:T(8,128)(2,1)}, u32[]{:S(2)}, u32[]{:S(2)}) collective-permute-start(bf16[128,8192]{1,0:T(8,128)(2,1)} %bitcast.20), channel_id=1, source_target_pairs={{0,64},{64,0},{1,65},{65,1},{2,66},{66,2},{3,67},{67,3},{4,68},{68... | collective-permute-start | bytes 6291464 | tf_op jit(solution)/shard_map/ppermute | solution.py:124
  36.2 2.4 %collective-permute-start.1 = (bf16[128,8192]{1,0:T(8,128)(2,1)}, bf16[128,8192]{1,0:T(8,128)(2,1)}, u32[]{:S(2)}, u32[]{:S(2)}) collective-permute-start(bf16[128,8192]{1,0:T(8,128)(2,1)} %bitcast.22), channel_id=1, source_target_pairs={{0,64},{64,0},{1,65},{65,1},{2,66},{66,2},{3,67},{67,3},{4,68},{68... | collective-permute-start | bytes 6291464 | tf_op jit(solution)/shard_map/ppermute | solution.py:125
  38.6 13.1 %all-to-all-done.3 = bf16[16,64,128]{2,1,0:T(8,128)(2,1)S(1)} async-done(((bf16[16,64,128]{2,1,0:T(8,128)(2,1)}), bf16[16,64,128]{2,1,0:T(8,128)(2,1)S(1)}, u32[]{:S(2)}, u32[]{:S(2)}) %all-to-all-start.3) | async-done | bytes 262176 | tf_op jit(solution)/shard_map/all_to_all | solution.py:17
  51.7 0.2 broadcast_in_dim.13
  51.9 18.7 %all_to_all.30 = bf16[16,16,16,128]{3,2,1,0:T(8,128)(2,1)S(1)} all-to-all(bf16[16,16,16,128]{3,2,1,0:T(8,128)(2,1)S(1)} %broadcast_in_dim.13), channel_id=1, replica_groups=mesh['x'=4,'c'=2,'y'=4,'z'=16] {'x','y'}, dimensions={0} | all-to-all | bytes 2097152 | tf_op jit(solution)/shard_map/all_to_all | solution.py:17
  70.6 1.2 broadcast_in_dim.16
  71.9 4.9 %all-to-all-start.4 = ((bf16[4,16,64,128]{3,2,1,0:T(8,128)(2,1)}), bf16[4,16,64,128]{3,2,1,0:T(8,128)(2,1)S(1)}, u32[]{:S(2)}, u32[]{:S(2)}) async-start(bf16[4,16,64,128]{3,2,1,0:T(8,128)(2,1)} %broadcast_in_dim.16), calls=%async_computation.4 | async-start | bytes 2097152 | tf_op jit(solution)/shard_map/all_to_all | solution.py:17
  76.8 0.0 collective-permute-done.act_par
  76.8 0.0 collective-permute-done.1.inc_par
  76.8 0.0 copy-start.1
  76.8 1.6 %copy-done.1 = bf16[1,128,8192]{2,1,0:T(8,128)(2,1)S(1)} copy-done((bf16[1,128,8192]{2,1,0:T(8,128)(2,1)S(1)}, bf16[1,128,8192]{2,1,0:T(8,128)(2,1)}, u32[]{:S(2)}) %copy-start.1) | copy-done | bytes 2097176
  78.4 0.0 copy-start.2
  78.4 1.6 %copy-done.2 = bf16[1,128,8192]{2,1,0:T(8,128)(2,1)S(1)} copy-done((bf16[1,128,8192]{2,1,0:T(8,128)(2,1)S(1)}, bf16[1,128,8192]{2,1,0:T(8,128)(2,1)}, u32[]{:S(2)}) %copy-start.2) | copy-done | bytes 2097176
  80.0 0.0 copy-start.3
  80.0 5.7 %shard_map.73 = f32[8,64,128]{2,1,0:T(8,128)} custom-call(bf16[4,4,16,16,128]{4,3,2,1,0:T(8,128)(2,1)S(1)} %bitcast.18, bf16[128,8192]{1,0:T(8,128)(2,1)S(1)} %bitcast.21, bf16[128,8192]{1,0:T(8,128)(2,1)} %collective-permute-done.act_par, bf16[128,8192]{1,0:T(8,128)(2,1)S(1)} %bitcast.23, bf16[128,8192]{1,0:T(8,128)(2,1)} %collective-permute-done.1.inc_par), custom_call_target="tpu_custom_call" | custom-call | flops 536870912 | bytes 9437184 | tf_op jit(solution)/shard_map/pallas_call | solution.py:57
  85.7 0.5 all-to-all-done.4
  86.2 3.4 %all-to-all-start.2 = ((f32[8,64,128]{2,1,0:T(8,128)}), f32[8,64,128]{2,1,0:T(8,128)S(1)}, u32[]{:S(2)}, u32[]{:S(2)}) async-start(f32[8,64,128]{2,1,0:T(8,128)} %shard_map.73), calls=%async_computation.2 | async-start | bytes 524288 | tf_op jit(solution)/shard_map/all_to_all | solution.py:128
  90.3 6.8 %all-to-all-done.2.parts_ref = f32[8,64,128]{2,1,0:T(8,128)S(1)} async-done(((f32[8,64,128]{2,1,0:T(8,128)}), f32[8,64,128]{2,1,0:T(8,128)S(1)}, u32[]{:S(2)}, u32[]{:S(2)}) %all-to-all-start.2) | async-done | bytes 262176 | tf_op jit(solution)/shard_map/all_to_all | solution.py:128
  97.1 1.4 %shard_map.74 = f32[64,128]{1,0:T(8,128)} custom-call(s32[1]{0:T(128)S(6)} %copy.12.len_ref, f32[8,64,128]{2,1,0:T(8,128)S(1)} %all-to-all-done.2.parts_ref, bf16[128,32,128]{2,1,0:T(8,128)(2,1)S(1)} %bitcast.19), custom_call_target="tpu_custom_call" | custom-call | flops 1048576 | bytes 1048576 | tf_op jit(solution)/shard_map/pallas_call | solution.py:101
  98.5 12.0 %all-to-all-start.5 = ((f32[64,1,128]{2,1,0:T(1,128)}), f32[64,1,128]{2,1,0:T(1,128)S(1)}, u32[]{:S(2)}, u32[]{:S(2)}) async-start(f32[64,1,128]{2,1,0:T(1,128)} %bitcast.6), calls=%async_computation.5 | async-start | bytes 65536 | tf_op jit(solution)/shard_map/all_to_all | solution.py:130
  110.5 0.0 copy-done.3
  110.6 13.4 %all-to-all-done.5 = f32[64,1,128]{2,1,0:T(1,128)S(1)} async-done(((f32[64,1,128]{2,1,0:T(1,128)}), f32[64,1,128]{2,1,0:T(1,128)S(1)}, u32[]{:S(2)}, u32[]{:S(2)}) %all-to-all-start.5) | async-done | bytes 32800 | tf_op jit(solution)/shard_map/all_to_all | solution.py:130
  124.0 0.1 broadcast_multiply_fusion
  124.1 0.9 convolution_bitcast_fusion
  (4 shorter events, 0.0 us)
Async XLA Ops:
  0.0 0.7 copy-start
  2.1 27.9 %all-to-all-start = ((bf16[16,16,128]{2,1,0:T(8,128)(2,1)}), bf16[16,16,128]{2,1,0:T(8,128)(2,1)S(1)}, u32[]{:S(2)}, u32[]{:S(2)}) async-start(bf16[16,16,128]{2,1,0:T(8,128)(2,1)} %broadcast_in_dim.12), calls=%async_computation | async-start | bytes 131072 | tf_op jit(solution)/shard_map/all_to_all | solution.py:17
  30.8 20.9 %all-to-all-start.3 = ((bf16[16,64,128]{2,1,0:T(8,128)(2,1)}), bf16[16,64,128]{2,1,0:T(8,128)(2,1)S(1)}, u32[]{:S(2)}, u32[]{:S(2)}) async-start(bf16[16,64,128]{2,1,0:T(8,128)(2,1)} %broadcast_in_dim.15), calls=%async_computation.3 | async-start | bytes 524288 | tf_op jit(solution)/shard_map/all_to_all | solution.py:17
  34.3 42.5 %collective-permute-start = (bf16[128,8192]{1,0:T(8,128)(2,1)}, bf16[128,8192]{1,0:T(8,128)(2,1)}, u32[]{:S(2)}, u32[]{:S(2)}) collective-permute-start(bf16[128,8192]{1,0:T(8,128)(2,1)} %bitcast.20), channel_id=1, source_target_pairs={{0,64},{64,0},{1,65},{65,1},{2,66},{66,2},{3,67},{67,3},{4,68},{68... | collective-permute-start | bytes 6291464 | tf_op jit(solution)/shard_map/ppermute | solution.py:124
  36.2 40.6 %collective-permute-start.1 = (bf16[128,8192]{1,0:T(8,128)(2,1)}, bf16[128,8192]{1,0:T(8,128)(2,1)}, u32[]{:S(2)}, u32[]{:S(2)}) collective-permute-start(bf16[128,8192]{1,0:T(8,128)(2,1)} %bitcast.22), channel_id=1, source_target_pairs={{0,64},{64,0},{1,65},{65,1},{2,66},{66,2},{3,67},{67,3},{4,68},{68... | collective-permute-start | bytes 6291464 | tf_op jit(solution)/shard_map/ppermute | solution.py:125
  71.9 14.4 %all-to-all-start.4 = ((bf16[4,16,64,128]{3,2,1,0:T(8,128)(2,1)}), bf16[4,16,64,128]{3,2,1,0:T(8,128)(2,1)S(1)}, u32[]{:S(2)}, u32[]{:S(2)}) async-start(bf16[4,16,64,128]{3,2,1,0:T(8,128)(2,1)} %broadcast_in_dim.16), calls=%async_computation.4 | async-start | bytes 2097152 | tf_op jit(solution)/shard_map/all_to_all | solution.py:17
  76.8 1.6 %copy-start.1 = (bf16[1,128,8192]{2,1,0:T(8,128)(2,1)S(1)}, bf16[1,128,8192]{2,1,0:T(8,128)(2,1)}, u32[]{:S(2)}) copy-start(bf16[1,128,8192]{2,1,0:T(8,128)(2,1)} %param.7) | copy-start | bytes 6291460
  78.4 1.6 %copy-start.2 = (bf16[1,128,8192]{2,1,0:T(8,128)(2,1)S(1)}, bf16[1,128,8192]{2,1,0:T(8,128)(2,1)}, u32[]{:S(2)}) copy-start(bf16[1,128,8192]{2,1,0:T(8,128)(2,1)} %param.8) | copy-start | bytes 6291460
  80.0 30.5 %copy-start.3 = (s32[64]{0:T(128)S(1)}, s32[64]{0:T(128)}, u32[]{:S(2)}) copy-start(s32[64]{0:T(128)} %param.13) | copy-start | bytes 772
  86.2 10.9 %all-to-all-start.2 = ((f32[8,64,128]{2,1,0:T(8,128)}), f32[8,64,128]{2,1,0:T(8,128)S(1)}, u32[]{:S(2)}, u32[]{:S(2)}) async-start(f32[8,64,128]{2,1,0:T(8,128)} %shard_map.73), calls=%async_computation.2 | async-start | bytes 524288 | tf_op jit(solution)/shard_map/all_to_all | solution.py:128
  98.5 25.4 %all-to-all-start.5 = ((f32[64,1,128]{2,1,0:T(1,128)}), f32[64,1,128]{2,1,0:T(1,128)S(1)}, u32[]{:S(2)}, u32[]{:S(2)}) async-start(f32[64,1,128]{2,1,0:T(1,128)} %bitcast.6), calls=%async_computation.5 | async-start | bytes 65536 | tf_op jit(solution)/shard_map/all_to_all | solution.py:130

commit v2 on v1

v2 whole, which is shorter than its diff:
```python
import jax
import jax.numpy as jnp
from jax import lax
from jax.experimental import pallas as pl
from jax.experimental.pallas import tpu as pltpu
from jax.sharding import Mesh
from jax.sharding import PartitionSpec as P

HIGHEST = lax.Precision.HIGHEST
NX, NC, NY, NZ = 4, 2, 4, 16
NT = (((1,), (1,)), ((), ()))
MIB = 2**20
f32, bf16 = jnp.float32, jnp.bfloat16
VMEM = pl.BlockSpec(memory_space=pltpu.VMEM)
SMEM = pl.BlockSpec(memory_space=pltpu.SMEM)


def params(mib=60):
    return pltpu.CompilerParams(vmem_limit_bytes=mib * MIB)


def cost(flops, moved):
    return pl.CostEstimate(flops=flops, bytes_accessed=moved, transcendentals=0)


def pack_kernel(in_ref, out_ref, valid_ref, sent_ref, proj_ref, rows_ref):
    x, c = lax.axis_index("x"), lax.axis_index("c")
    proj_ref[0] = in_ref[...].astype(f32)
    proj_ref[1] = out_ref[...].astype(f32)
    rows_ref[0:8] = proj_ref[0, pl.ds(c * 32 + x * 8, 8)]
    rows_ref[8:16] = proj_ref[1, pl.ds(x * 16 + c, 8, stride=2)]
    for r in range(32):
        pair = valid_ref[0, :, r * 128 : (r + 1) * 128].astype(f32)
        rows_ref[16 + r : 17 + r] = pair[0:1]
        rows_ref[48 + r : 49 + r] = pair[1:2]
    sent_ref[...] = jnp.broadcast_to(rows_ref[...].astype(bf16)[None], (NZ, 80, 128))


def pack(proj_in, proj_out, valid_rows):
    return pl.pallas_call(
        pack_kernel,
        out_shape=pltpu.HBM((NZ, 80, 128), bf16),
        in_specs=[VMEM] * 3,
        out_specs=VMEM,
        scratch_shapes=[pltpu.VMEM((2, 64, 128), f32), pltpu.VMEM((80, 128), f32)],
        compiler_params=params(32),
        cost_estimate=cost(0, 368 * 1024),
    )(*in_hbm(proj_in, proj_out, valid_rows))


def split_kernel(got_ref, proj_ref, valid_ref):
    proj_ref[...] = jnp.broadcast_to(got_ref[:, 0:16][None], (NX * NY, NZ, 16, 128))
    valid_ref[...] = got_ref[:, 16:80]


def split(got):
    return pl.pallas_call(
        split_kernel,
        out_shape=(
            pltpu.HBM((NX * NY, NZ, 16, 128), bf16),
            jax.ShapeDtypeStruct((NZ, 64, 128), bf16),
        ),
        in_specs=[VMEM],
        out_specs=(VMEM, VMEM),
        compiler_params=params(32),
        cost_estimate=cost(0, 1536 * 1024),
    )(got)


def project_half(w_ref, own_ref, par_ref, data_ref, sems):
    wide = own_ref.shape[1] // 2
    copies = []
    for half in range(2):
        for k, ref in enumerate((own_ref, par_ref)):
            copy = pltpu.make_async_copy(
                ref.at[:, pl.ds(half * wide, wide)],
                data_ref.at[pl.ds(k * 128, 128), pl.ds(half * wide, wide)],
                sems.at[half, k],
            )
            copy.start()
            copies.append(copy)
    total = None
    for half in range(2):
        w = jnp.concatenate(
            [
                w_ref[:, y, z].reshape(NX * 16, 128)
                for y in range(2 * half, 2 * half + 2)
                for z in range(NZ)
            ],
            axis=1,
        )
        copies[2 * half].wait()
        copies[2 * half + 1].wait()
        part = lax.dot_general(
            w, data_ref[:, half * wide : (half + 1) * wide], NT, preferred_element_type=f32
        )
        total = part if total is None else total + part
    return total


def half_rows(value, which):
    return value.reshape(NX, 2, 8, value.shape[1])[:, which].reshape(32, value.shape[1])


def grad_kernel(w_ref, own_ref, par_ref, out_ref, data_ref, sems):
    total = half_rows(project_half(w_ref, own_ref, par_ref, data_ref, sems), 1)
    my_x, my_c = lax.axis_index("x"), lax.axis_index("c")
    own, par = total[:, 0:128], total[:, 128:256]
    pair = own + par
    odd = jnp.where(my_c == 1, own, par)
    zero = jnp.zeros_like(pair)
    for x in range(NX):
        upper = jnp.where(x < my_x, pair, zero)
        out_ref[x * NC] = jnp.where(x == my_x, pair, upper)
        out_ref[x * NC + 1] = jnp.where(x == my_x, odd, upper)


def act_kernel(w_ref, own_ref, par_ref, mine_ref, theirs_ref, data_ref, sems):
    total = half_rows(project_half(w_ref, own_ref, par_ref, data_ref, sems), 0)
    mine_ref[...] = total[:, 0:128]
    theirs_ref[...] = total[:, 128:256]


def in_hbm(*arrays):
    return [pltpu.with_memory_space_constraint(a, pltpu.HBM) for a in arrays]


FETCH = [pltpu.VMEM((256, 8192), bf16), pltpu.SemaphoreType.DMA((2, 2))]
HBM = pl.BlockSpec(memory_space=pltpu.HBM)


def project_grads(w, own, par):
    return pl.pallas_call(
        grad_kernel,
        out_shape=pltpu.HBM((NX * NC, 32, 128), f32),
        in_specs=[VMEM, HBM, HBM],
        out_specs=VMEM,
        scratch_shapes=FETCH,
        compiler_params=params(24),
        cost_estimate=cost(2 * 256 * 8192 * 64, 5 * MIB),
    )(w, *in_hbm(own, par))


def project_acts(w, own, par):
    return pl.pallas_call(
        act_kernel,
        out_shape=(jax.ShapeDtypeStruct((32, 128), f32), pltpu.HBM((32, 128), f32)),
        in_specs=[VMEM, HBM, HBM],
        out_specs=(VMEM, VMEM),
        scratch_shapes=FETCH,
        compiler_params=params(24),
        cost_estimate=cost(2 * 256 * 8192 * 64, 5 * MIB),
    )(w, *in_hbm(own, par))


def score_kernel(len_ref, parts_ref, mine_ref, theirs_ref, *refs):
    valid_refs, out_ref = refs[:NY], refs[NY]
    my_c, my_y = lax.axis_index("c"), lax.axis_index("y")
    live = len_ref[0]
    tok = lax.broadcasted_iota(jnp.int32, (32, 128), 1)
    weight = jnp.where(tok < live, 1.0, 0.0).astype(f32) / live.astype(f32)
    mine, theirs = mine_ref[...], theirs_ref[...]
    act = jnp.concatenate(
        [jnp.where(my_c == 0, mine, theirs), jnp.where(my_c == 0, theirs, mine)], axis=0
    )
    halves = []
    for c in range(NC):
        total = parts_ref[c]
        for x in range(1, NX):
            total = total + parts_ref[x * NC + c]
        halves.append(
            lax.dot_general(
                total * weight, act, NT, precision=HIGHEST, preferred_element_type=f32
            )
        )
    row = jnp.concatenate(halves, axis=1).astype(bf16).astype(f32)
    for k, valid_ref in enumerate(valid_refs):
        part = jnp.sum(valid_ref[...].astype(f32) * row[None], axis=1)
        scores = lax.dot_general(
            jnp.ones((64, 128), f32), part, NT, precision=HIGHEST, preferred_element_type=f32
        )
        place = lax.rem(my_y - k + NY, NY)
        for y in range(NY):

            @pl.when(place == y)
            def _():
                out_ref[:, y * 32 : (y + 1) * 32] = scores


def score(lengths, parts, mine, theirs, valid):
    return pl.pallas_call(
        score_kernel,
        out_shape=pltpu.HBM((64, 128), f32),
        in_specs=[SMEM] + [VMEM] * (3 + NY),
        out_specs=VMEM,
        compiler_params=params(32),
        cost_estimate=cost(2 * 128 * 4096, MIB),
    )(lengths, parts, mine, theirs, *valid)


def gram_kernel(dom_ref, scores_ref, out_ref):
    me = lax.axis_index("y") * NZ + lax.axis_index("z")
    scores = scores_ref[...]
    owned = jnp.where(dom_ref[...] == me, 1.0, 0.0).astype(f32)
    out_ref[...] = jnp.dot(
        scores.T * owned, scores, precision=HIGHEST, preferred_element_type=f32
    )


def gram(domains, scores):
    return pl.pallas_call(
        gram_kernel,
        out_shape=jax.ShapeDtypeStruct((128, 128), f32),
        in_specs=[VMEM, VMEM],
        out_specs=VMEM,
        compiler_params=params(24),
        cost_estimate=cost(2 * 128 * 128 * 64 * 6, 96 * 1024),
    )(domains, scores)


def body(acts, incoming, proj_in, proj_out, valid_rows, lengths, domains):
    swap = [(0, 1), (1, 0)]
    act_own, inc_own = acts[0], incoming[0]
    got = lax.all_to_all(pack(proj_in, proj_out, valid_rows), "z", 0, 0)
    inc_par = lax.ppermute(inc_own, "c", swap)
    act_par = lax.ppermute(act_own, "c", swap)
    sent, valid_here = split(got)
    w = lax.all_to_all(sent, ("x", "y"), 0, 0).reshape(NX, NY, NZ, 16, 128)
    valid = [valid_here] + [
        lax.ppermute(valid_here, "y", [(i, (i + k) % NY) for i in range(NY)]) for k in range(1, NY)
    ]
    parts = lax.all_to_all(project_grads(w, inc_own, inc_par), ("x", "c"), 0, 0)
    mine, others = project_acts(w, act_own, act_par)
    theirs = lax.ppermute(others, "c", swap)
    scores = score(lengths, parts, mine, theirs, [v.reshape(32, 32, 128) for v in valid])
    scores = lax.all_to_all(scores.reshape(64, 1, 128), ("y", "z"), 0, 0).reshape(64, 128)
    return gram(domains.reshape(1, 64), scores)[None, None]


def solution(mesh):
    fine = Mesh(mesh.devices.reshape(NX, NC, NY, NZ), ("x", "c", "y", "z"))
    pipe, dp = ("x", "c"), ("y", "z")
    placed = (
        P(pipe, dp, None),
        P(pipe, dp, None),
        P(None, dp),
        P(None, dp),
        P(pipe, dp, None),
        P(dp),
        P(),
    )
    return jax.shard_map(
        body, mesh=fine, in_specs=placed, out_specs=P(pipe, dp, None, None), check_vma=False
    )
```

time: 126 us -> 105 us (0.83)
  the two profiles are of different devices: /device:TPU:8 before, /device:TPU:2 now
where the time goes in v2:
time: 105 us
  starting transfers between devices  45.4 us (43%)
  blocking collectives  27.4 us (26%)
  waiting for transfers between devices  17 us (16%)
  Pallas kernels  14.2 us (14%)
    all_to_all x1, blocking collectives, body(): lax.all_to_all(scores.reshape(64, 1, 128), ('y', 'z'), 0, 0)  27.4 us
    all_to_all x1, waiting for transfers between devices, body(): got = lax.all_to_all(pack(proj_in, proj_out, valid_rows), 'z', 0, 0)  16.4 us
    all_to_all x1, starting transfers between devices, body(): got = lax.all_to_all(pack(proj_in, proj_out, valid_rows), 'z', 0, 0)  15.2 us
    ppermute x3, starting transfers between devices, body(): lax.ppermute(valid_here, 'y', [(i, (i + k) % NY) for i in range(NY)])  11.3 us
    all_to_all x1, starting transfers between devices, body(): w = lax.all_to_all(sent, ('x', 'y'), 0, 0).reshape(NX, NY, NZ, 16, 128)  7.48 us
    all_to_all x1, starting transfers between devices, body(): parts = lax.all_to_all(project_grads(w, inc_own, inc_par), ('x', 'c'), 0, 0)  5.06 us
    pallas_call x1, Pallas kernels, project_grads(): pl.pallas_call(grad_kernel, out_shape=pltpu.HBM((NX * NC, 32, 128), f32),...  4.24 us
    pallas_call x1, Pallas kernels, project_acts(): pl.pallas_call(act_kernel, out_shape=(jax.ShapeDtypeStruct((32, 128), f32...  4.19 us
  transfers between devices with their start and end apart: 9, of which 2 were waited for; matrix products, arithmetic and copies ran while one was open for 0% of the time, Pallas kernels for 9%

profile of v2, /device:TPU:2, one launch (start us, length us, event | category | flops | bytes accessed | tf_op | source)
XLA Modules:
  0.0 104.7 jit_solution(15830166925032453150)
XLA Ops:
  0.0 1.5 %shard_map.73 = bf16[16,80,128]{2,1,0:T(8,128)(2,1)} custom-call(bf16[64,128]{1,0:T(8,128)(2,1)} %in_ref.1, bf16[64,128]{1,0:T(8,128)(2,1)} %out_ref.1, bf16[1,2,4096]{2,1,0:T(2,128)(2,1)} %valid_ref.1), custom_call_target="tpu_custom_call" | custom-call | bytes 376832 | tf_op jit(solution)/shard_map/pallas_call | solution.py:40
  1.5 15.2 %all-to-all-start = ((bf16[16,80,128]{2,1,0:T(8,128)(2,1)}), bf16[16,80,128]{2,1,0:T(8,128)(2,1)S(1)}, u32[]{:S(2)}, u32[]{:S(2)}) async-start(bf16[16,80,128]{2,1,0:T(8,128)(2,1)} %shard_map.73), calls=%async_computation | async-start | bytes 655360 | tf_op jit(solution)/shard_map/all_to_all | solution.py:224
  16.7 1.9 %collective-permute-start = (bf16[128,8192]{1,0:T(8,128)(2,1)}, bf16[128,8192]{1,0:T(8,128)(2,1)}, u32[]{:S(2)}, u32[]{:S(2)}) collective-permute-start(bf16[128,8192]{1,0:T(8,128)(2,1)} %bitcast.23), channel_id=1, source_target_pairs={{0,64},{64,0},{1,65},{65,1},{2,66},{66,2},{3,67},{67,3},{4,68},{68... | collective-permute-start | bytes 6291464 | tf_op jit(solution)/shard_map/ppermute | solution.py:225
  18.7 2.4 %collective-permute-start.1 = (bf16[128,8192]{1,0:T(8,128)(2,1)}, bf16[128,8192]{1,0:T(8,128)(2,1)}, u32[]{:S(2)}, u32[]{:S(2)}) collective-permute-start(bf16[128,8192]{1,0:T(8,128)(2,1)} %bitcast.21), channel_id=1, source_target_pairs={{0,64},{64,0},{1,65},{65,1},{2,66},{66,2},{3,67},{67,3},{4,68},{68... | collective-permute-start | bytes 6291464 | tf_op jit(solution)/shard_map/ppermute | solution.py:226
  21.1 16.4 %all-to-all-done.got_ref = bf16[16,80,128]{2,1,0:T(8,128)(2,1)S(1)} async-done(((bf16[16,80,128]{2,1,0:T(8,128)(2,1)}), bf16[16,80,128]{2,1,0:T(8,128)(2,1)S(1)}, u32[]{:S(2)}, u32[]{:S(2)}) %all-to-all-start) | async-done | bytes 327712 | tf_op jit(solution)/shard_map/all_to_all | solution.py:224
  37.5 1.2 %shard_map.74 = (bf16[16,16,16,128]{3,2,1,0:T(8,128)(2,1)}, bf16[16,64,128]{2,1,0:T(8,128)(2,1)S(1)}) custom-call(bf16[16,80,128]{2,1,0:T(8,128)(2,1)S(1)} %all-to-all-done.got_ref), custom_call_target="tpu_custom_call" | custom-call | bytes 1572864 | tf_op jit(solution)/shard_map/pallas_call | solution.py:57
  38.7 7.5 %all-to-all-start.1 = ((bf16[16,16,16,128]{3,2,1,0:T(8,128)(2,1)}), bf16[16,16,16,128]{3,2,1,0:T(8,128)(2,1)S(1)}, u32[]{:S(2)}, u32[]{:S(2)}) async-start(bf16[16,16,16,128]{3,2,1,0:T(8,128)(2,1)} %get-tuple-element.9), calls=%async_computation.1 | async-start | bytes 2097152 | tf_op jit(solution)/shard_map/all_to_all | solution.py:228
  46.2 3.4 %collective-permute-start.3 = (bf16[16,64,128]{2,1,0:T(8,128)(2,1)S(1)}, bf16[16,64,128]{2,1,0:T(8,128)(2,1)S(1)}, u32[]{:S(2)}, u32[]{:S(2)}) collective-permute-start(bf16[16,64,128]{2,1,0:T(8,128)(2,1)S(1)} %get-tuple-element.12), channel_id=1, source_target_pairs={{0,16},{16,32},{32,48},{48,0},{1,17},{17,33},{33,49},{49,1},{2,18}... | collective-permute-start | bytes 786440 | tf_op jit(solution)/shard_map/ppermute | solution.py:230
  49.5 4.6 %collective-permute-start.4 = (bf16[16,64,128]{2,1,0:T(8,128)(2,1)S(1)}, bf16[16,64,128]{2,1,0:T(8,128)(2,1)S(1)}, u32[]{:S(2)}, u32[]{:S(2)}) collective-permute-start(bf16[16,64,128]{2,1,0:T(8,128)(2,1)S(1)} %get-tuple-element.12), channel_id=1, source_target_pairs={{0,32},{16,48},{32,0},{48,16},{1,33},{17,49},{33,1},{49,17},{2,34}... | collective-permute-start | bytes 786440 | tf_op jit(solution)/shard_map/ppermute | solution.py:230
  54.1 3.4 %collective-permute-start.5 = (bf16[16,64,128]{2,1,0:T(8,128)(2,1)S(1)}, bf16[16,64,128]{2,1,0:T(8,128)(2,1)S(1)}, u32[]{:S(2)}, u32[]{:S(2)}) collective-permute-start(bf16[16,64,128]{2,1,0:T(8,128)(2,1)S(1)} %get-tuple-element.12), channel_id=1, source_target_pairs={{0,48},{16,0},{32,16},{48,32},{1,49},{17,1},{33,17},{49,33},{2,50}... | collective-permute-start | bytes 786440 | tf_op jit(solution)/shard_map/ppermute | solution.py:230
  57.5 0.0 collective-permute-done.par_ref
  57.5 0.0 all-to-all-done.1
  57.5 4.2 %shard_map.75 = f32[8,32,128]{2,1,0:T(8,128)} custom-call(bf16[4,4,16,16,128]{4,3,2,1,0:T(8,128)(2,1)S(1)} %bitcast.13, bf16[128,8192]{1,0:T(8,128)(2,1)} %bitcast.24, bf16[128,8192]{1,0:T(8,128)(2,1)} %collective-permute-done.par_ref), custom_call_target="tpu_custom_call" | custom-call | flops 268435456 | bytes 5242880 | tf_op jit(solution)/shard_map/pallas_call | solution.py:133
  61.8 5.1 %all-to-all-start.2 = ((f32[8,32,128]{2,1,0:T(8,128)}), f32[8,32,128]{2,1,0:T(8,128)S(1)}, u32[]{:S(2)}, u32[]{:S(2)}) async-start(f32[8,32,128]{2,1,0:T(8,128)} %shard_map.75), calls=%async_computation.2 | async-start | bytes 262144 | tf_op jit(solution)/shard_map/all_to_all | solution.py:232
  66.9 0.0 copy-start
  66.9 0.0 collective-permute-done.1.par_ref
  66.9 4.2 %shard_map.76 = (f32[32,128]{1,0:T(8,128)S(1)}, f32[32,128]{1,0:T(8,128)}) custom-call(bf16[4,4,16,16,128]{4,3,2,1,0:T(8,128)(2,1)S(1)} %bitcast.14, bf16[128,8192]{1,0:T(8,128)(2,1)} %bitcast.22, bf16[128,8192]{1,0:T(8,128)(2,1)} %collective-permute-done.1.par_ref), custom_call_target="tpu_custom_call" | custom-call | flops 268435456 | bytes 5242880 | tf_op jit(solution)/shard_map/pallas_call | solution.py:145
  71.1 2.1 %collective-permute-start.2 = (f32[32,128]{1,0:T(8,128)}, f32[32,128]{1,0:T(8,128)S(1)}, u32[]{:S(2)}, u32[]{:S(2)}) collective-permute-start(f32[32,128]{1,0:T(8,128)} %get-tuple-element.11), channel_id=1, source_target_pairs={{0,64},{64,0},{1,65},{65,1},{2,66},{66,2},{3,67},{67,3},{4,68},{68... | collective-permute-start | bytes 49160 | tf_op jit(solution)/shard_map/ppermute | solution.py:234
  73.8 0.0 collective-permute-done.3
  73.8 0.0 collective-permute-done.4
  73.8 0.0 collective-permute-done.5
  73.8 0.5 collective-permute-done.2.theirs_ref
  74.4 0.0 all-to-all-done.2.parts_ref
  74.4 2.1 %shard_map.77 = f32[64,128]{1,0:T(8,128)} custom-call(s32[1]{0:T(128)S(6)} %copy.9.len_ref, f32[8,32,128]{2,1,0:T(8,128)S(1)} %all-to-all-done.2.parts_ref, f32[32,128]{1,0:T(8,128)S(1)} %get-tuple-element.10.mine_ref, f32[32,128]{1,0:T(8,128)S(1)} %collective-permute-done.2.theirs_ref, bf16[32,32,128]{2,1,0:T(8,128)(2,1)S(1)} %bitcast.15, ...), custom_call_target="tpu_custom_call" | custom-call | flops 1048576 | bytes 1048576 | tf_op jit(solution)/shard_map/pallas_call | solution.py:191
  76.5 27.4 %all_to_all.20 = f32[64,1,128]{2,1,0:T(1,128)S(1)} all-to-all(f32[64,1,128]{2,1,0:T(1,128)} %bitcast.25), channel_id=1, replica_groups=mesh['x'=4,'c'=2,'y'=4,'z'=16] {'y','z'}, dimensions={0} | all-to-all | bytes 65536 | tf_op jit(solution)/shard_map/all_to_all | solution.py:236
  103.8 0.0 copy-done
  103.8 0.9 shard_map.78
Async XLA Ops:
  1.5 36.0 %all-to-all-start = ((bf16[16,80,128]{2,1,0:T(8,128)(2,1)}), bf16[16,80,128]{2,1,0:T(8,128)(2,1)S(1)}, u32[]{:S(2)}, u32[]{:S(2)}) async-start(bf16[16,80,128]{2,1,0:T(8,128)(2,1)} %shard_map.73), calls=%async_computation | async-start | bytes 655360 | tf_op jit(solution)/shard_map/all_to_all | solution.py:224
  16.7 40.8 %collective-permute-start = (bf16[128,8192]{1,0:T(8,128)(2,1)}, bf16[128,8192]{1,0:T(8,128)(2,1)}, u32[]{:S(2)}, u32[]{:S(2)}) collective-permute-start(bf16[128,8192]{1,0:T(8,128)(2,1)} %bitcast.23), channel_id=1, source_target_pairs={{0,64},{64,0},{1,65},{65,1},{2,66},{66,2},{3,67},{67,3},{4,68},{68... | collective-permute-start | bytes 6291464 | tf_op jit(solution)/shard_map/ppermute | solution.py:225
  18.7 48.2 %collective-permute-start.1 = (bf16[128,8192]{1,0:T(8,128)(2,1)}, bf16[128,8192]{1,0:T(8,128)(2,1)}, u32[]{:S(2)}, u32[]{:S(2)}) collective-permute-start(bf16[128,8192]{1,0:T(8,128)(2,1)} %bitcast.21), channel_id=1, source_target_pairs={{0,64},{64,0},{1,65},{65,1},{2,66},{66,2},{3,67},{67,3},{4,68},{68... | collective-permute-start | bytes 6291464 | tf_op jit(solution)/shard_map/ppermute | solution.py:226
  38.7 18.8 %all-to-all-start.1 = ((bf16[16,16,16,128]{3,2,1,0:T(8,128)(2,1)}), bf16[16,16,16,128]{3,2,1,0:T(8,128)(2,1)S(1)}, u32[]{:S(2)}, u32[]{:S(2)}) async-start(bf16[16,16,16,128]{3,2,1,0:T(8,128)(2,1)} %get-tuple-element.9), calls=%async_computation.1 | async-start | bytes 2097152 | tf_op jit(solution)/shard_map/all_to_all | solution.py:228
  46.2 27.6 %collective-permute-start.3 = (bf16[16,64,128]{2,1,0:T(8,128)(2,1)S(1)}, bf16[16,64,128]{2,1,0:T(8,128)(2,1)S(1)}, u32[]{:S(2)}, u32[]{:S(2)}) collective-permute-start(bf16[16,64,128]{2,1,0:T(8,128)(2,1)S(1)} %get-tuple-element.12), channel_id=1, source_target_pairs={{0,16},{16,32},{32,48},{48,0},{1,17},{17,33},{33,49},{49,1},{2,18}... | collective-permute-start | bytes 786440 | tf_op jit(solution)/shard_map/ppermute | solution.py:230
  49.5 24.2 %collective-permute-start.4 = (bf16[16,64,128]{2,1,0:T(8,128)(2,1)S(1)}, bf16[16,64,128]{2,1,0:T(8,128)(2,1)S(1)}, u32[]{:S(2)}, u32[]{:S(2)}) collective-permute-start(bf16[16,64,128]{2,1,0:T(8,128)(2,1)S(1)} %get-tuple-element.12), channel_id=1, source_target_pairs={{0,32},{16,48},{32,0},{48,16},{1,33},{17,49},{33,1},{49,17},{2,34}... | collective-permute-start | bytes 786440 | tf_op jit(solution)/shard_map/ppermute | solution.py:230
  54.1 19.7 %collective-permute-start.5 = (bf16[16,64,128]{2,1,0:T(8,128)(2,1)S(1)}, bf16[16,64,128]{2,1,0:T(8,128)(2,1)S(1)}, u32[]{:S(2)}, u32[]{:S(2)}) collective-permute-start(bf16[16,64,128]{2,1,0:T(8,128)(2,1)S(1)} %get-tuple-element.12), channel_id=1, source_target_pairs={{0,48},{16,0},{32,16},{48,32},{1,49},{17,1},{33,17},{49,33},{2,50}... | collective-permute-start | bytes 786440 | tf_op jit(solution)/shard_map/ppermute | solution.py:230
  61.8 12.6 %all-to-all-start.2 = ((f32[8,32,128]{2,1,0:T(8,128)}), f32[8,32,128]{2,1,0:T(8,128)S(1)}, u32[]{:S(2)}, u32[]{:S(2)}) async-start(f32[8,32,128]{2,1,0:T(8,128)} %shard_map.75), calls=%async_computation.2 | async-start | bytes 262144 | tf_op jit(solution)/shard_map/all_to_all | solution.py:232
  66.9 37.0 %copy-start = (s32[64]{0:T(128)S(1)}, s32[64]{0:T(128)}, u32[]{:S(2)}) copy-start(s32[64]{0:T(128)} %param.13) | copy-start | bytes 772
  71.1 3.3 %collective-permute-start.2 = (f32[32,128]{1,0:T(8,128)}, f32[32,128]{1,0:T(8,128)S(1)}, u32[]{:S(2)}, u32[]{:S(2)}) collective-permute-start(f32[32,128]{1,0:T(8,128)} %get-tuple-element.11), channel_id=1, source_target_pairs={{0,64},{64,0},{1,65},{65,1},{2,66},{66,2},{3,67},{67,3},{4,68},{68... | collective-permute-start | bytes 49160 | tf_op jit(solution)/shard_map/ppermute | solution.py:234

commit v3 on v2

v3 whole, which is shorter than its diff:
```python
import jax
import jax.numpy as jnp
from jax import lax
from jax.experimental import pallas as pl
from jax.experimental.pallas import tpu as pltpu
from jax.sharding import Mesh
from jax.sharding import PartitionSpec as P

HIGHEST = lax.Precision.HIGHEST
AXES = ("x", "c", "y", "u", "p")
SIZES = NX, NC, NY, NU, NP = 4, 2, 4, 8, 2
NT = (((1,), (1,)), ((), ()))
MIB = 2**20
f32, bf16 = jnp.float32, jnp.bfloat16
VMEM = pl.BlockSpec(memory_space=pltpu.VMEM)
SMEM = pl.BlockSpec(memory_space=pltpu.SMEM)
HBM = pl.BlockSpec(memory_space=pltpu.HBM)


def in_hbm(*arrays):
    return [pltpu.with_memory_space_constraint(a, pltpu.HBM) for a in arrays]


def params(mib):
    return pltpu.CompilerParams(vmem_limit_bytes=mib * MIB)


def cost(flops, moved):
    return pl.CostEstimate(flops=flops, bytes_accessed=moved, transcendentals=0)


def pack_kernel(in_ref, out_ref, valid_ref, sent_ref, proj_ref, rows_ref):
    c = lax.axis_index("c")
    proj_ref[0] = in_ref[...].astype(f32)
    proj_ref[1] = out_ref[...].astype(f32)
    rows_ref[0:32] = proj_ref[0, pl.ds(pl.multiple_of(c * 32, 32), 32)]
    rows_ref[32:64] = proj_ref[1, pl.ds(c, 32, stride=2)]
    for r in range(32):
        pair = valid_ref[0, :, r * 128 : (r + 1) * 128].astype(f32)
        rows_ref[64 + r : 65 + r] = pair[0:1]
        rows_ref[96 + r : 97 + r] = pair[1:2]
    sent_ref[...] = jnp.broadcast_to(rows_ref[...].astype(bf16)[None], (NU, 128, 128))


def pack(proj_in, proj_out, valid_rows):
    return pl.pallas_call(
        pack_kernel,
        out_shape=pltpu.HBM((NU, 128, 128), bf16),
        in_specs=[VMEM] * 3,
        out_specs=VMEM,
        scratch_shapes=[pltpu.VMEM((2, 64, 128), f32), pltpu.VMEM((128, 128), f32)],
        compiler_params=params(32),
        cost_estimate=cost(0, 304 * 1024),
    )(*in_hbm(proj_in, proj_out, valid_rows))


def split_kernel(got_ref, proj_ref, valid_ref):
    proj_ref[...] = jnp.broadcast_to(got_ref[:, 0:64][None], (NY * NP, NU, 64, 128))
    valid_ref[...] = got_ref[:, 64:128]


def split(got):
    return pl.pallas_call(
        split_kernel,
        out_shape=(
            pltpu.HBM((NY * NP, NU, 64, 128), bf16),
            jax.ShapeDtypeStruct((NU, 64, 128), bf16),
        ),
        in_specs=[VMEM],
        out_specs=(VMEM, VMEM),
        compiler_params=params(32),
        cost_estimate=cost(0, 1536 * 1024),
    )(got)


def merge_kernel(*refs):
    for k in range(NY):
        refs[NY][k] = refs[k][...]


def merge(parts):
    return pl.pallas_call(
        merge_kernel,
        out_shape=jax.ShapeDtypeStruct((NY, NU, 64, 128), bf16),
        in_specs=[VMEM] * NY,
        out_specs=VMEM,
        compiler_params=params(32),
        cost_estimate=cost(0, MIB),
    )(*parts)


def project_half(which, w_ref, own_ref, par_ref, data_ref, sems):
    wide = own_ref.shape[1] // 2
    copies = []
    for half in range(2):
        for k, ref in enumerate((own_ref, par_ref)):
            copy = pltpu.make_async_copy(
                ref.at[:, pl.ds(half * wide, wide)],
                data_ref.at[pl.ds(k * 128, 128), pl.ds(half * wide, wide)],
                sems.at[half, k],
            )
            copy.start()
            copies.append(copy)
    total = None
    for half in range(2):
        w = jnp.concatenate(
            [
                w_ref[y, p, u, which * 32 : which * 32 + 32]
                for y in range(2 * half, 2 * half + 2)
                for u in range(NU)
                for p in range(NP)
            ],
            axis=1,
        )
        copies[2 * half].wait()
        copies[2 * half + 1].wait()
        part = lax.dot_general(
            w, data_ref[:, half * wide : (half + 1) * wide], NT, preferred_element_type=f32
        )
        total = part if total is None else total + part
    return total[:, 0:128], total[:, 128:256]


def grad_kernel(w_ref, own_ref, par_ref, out_ref, data_ref, sems):
    own, par = project_half(1, w_ref, own_ref, par_ref, data_ref, sems)
    my_x, my_c = lax.axis_index("x"), lax.axis_index("c")
    pair = own + par
    odd = jnp.where(my_c == 1, own, par)
    zero = jnp.zeros_like(pair)
    for x in range(NX):
        upper = jnp.where(x < my_x, pair, zero)
        out_ref[x * NC] = jnp.where(x == my_x, pair, upper)
        out_ref[x * NC + 1] = jnp.where(x == my_x, odd, upper)


def act_kernel(w_ref, own_ref, par_ref, mine_ref, theirs_ref, data_ref, sems):
    mine_ref[...], theirs_ref[...] = project_half(0, w_ref, own_ref, par_ref, data_ref, sems)


FETCH = [pltpu.VMEM((256, 8192), bf16), pltpu.SemaphoreType.DMA((2, 2))]


def project_grads(w, own, par):
    return pl.pallas_call(
        grad_kernel,
        out_shape=pltpu.HBM((NX * NC, 32, 128), f32),
        in_specs=[VMEM, HBM, HBM],
        out_specs=VMEM,
        scratch_shapes=FETCH,
        compiler_params=params(24),
        cost_estimate=cost(2 * 256 * 8192 * 64, 5 * MIB),
    )(w, *in_hbm(own, par))


def project_acts(w, own, par):
    return pl.pallas_call(
        act_kernel,
        out_shape=(jax.ShapeDtypeStruct((32, 128), f32), pltpu.HBM((32, 128), f32)),
        in_specs=[VMEM, HBM, HBM],
        out_specs=(VMEM, VMEM),
        scratch_shapes=FETCH,
        compiler_params=params(24),
        cost_estimate=cost(2 * 256 * 8192 * 64, 5 * MIB),
    )(w, *in_hbm(own, par))


def score_kernel(len_ref, parts_ref, mine_ref, theirs_ref, here_ref, there_ref, out_ref):
    my_c, my_y, my_p = lax.axis_index("c"), lax.axis_index("y"), lax.axis_index("p")
    live = len_ref[0]
    tok = lax.broadcasted_iota(jnp.int32, (32, 128), 1)
    weight = jnp.where(tok < live, 1.0, 0.0).astype(f32) / live.astype(f32)
    mine, theirs = mine_ref[...], theirs_ref[...]
    act = jnp.concatenate(
        [jnp.where(my_c == 0, mine, theirs), jnp.where(my_c == 0, theirs, mine)], axis=0
    )
    halves = []
    for c in range(NC):
        total = parts_ref[c]
        for x in range(1, NX):
            total = total + parts_ref[x * NC + c]
        halves.append(
            lax.dot_general(
                total * weight, act, NT, precision=HIGHEST, preferred_element_type=f32
            )
        )
    row = jnp.concatenate(halves, axis=1).astype(bf16).astype(f32)
    part = jnp.concatenate(
        [
            jnp.sum(ref[...].reshape(64, 32, 128).astype(f32) * row[None], axis=1)
            for ref in (here_ref, there_ref)
        ],
        axis=0,
    )
    came = lax.broadcasted_iota(jnp.int32, (128, 128), 0)
    y = (my_y + 4 - ((came >> 4) & 3)) & 3
    p = (my_p + (came >> 6)) & 1
    goes = y * 32 + ((came >> 1) & 7) * 4 + p * 2 + (came & 1)
    order = jnp.where(goes == lax.broadcasted_iota(jnp.int32, (128, 128), 1), 1.0, 0.0)
    scores = lax.dot_general(
        jnp.ones((64, 128), f32), part, NT, precision=HIGHEST, preferred_element_type=f32
    )
    out_ref[...] = jnp.dot(
        scores, order.astype(f32), precision=HIGHEST, preferred_element_type=f32
    )


def score(lengths, parts, mine, theirs, here, there):
    return pl.pallas_call(
        score_kernel,
        out_shape=pltpu.HBM((64, 128), f32),
        in_specs=[SMEM] + [VMEM] * 5,
        out_specs=VMEM,
        compiler_params=params(32),
        cost_estimate=cost(2 * 128 * 4096, MIB),
    )(lengths, parts, mine, theirs, here, there)


def gram_kernel(dom_ref, scores_ref, out_ref):
    me = lax.axis_index("y") * (NU * NP) + lax.axis_index("u") * NP + lax.axis_index("p")
    scores = scores_ref[...]
    owned = jnp.where(dom_ref[...] == me, 1.0, 0.0).astype(f32)
    out_ref[...] = jnp.dot(
        scores.T * owned, scores, precision=HIGHEST, preferred_element_type=f32
    )


def gram(domains, scores):
    return pl.pallas_call(
        gram_kernel,
        out_shape=jax.ShapeDtypeStruct((128, 128), f32),
        in_specs=[VMEM, VMEM],
        out_specs=VMEM,
        compiler_params=params(24),
        cost_estimate=cost(2 * 128 * 128 * 64 * 6, 96 * 1024),
    )(domains, scores)


def body(acts, incoming, proj_in, proj_out, valid_rows, lengths, domains):
    swap = [(0, 1), (1, 0)]
    act_own, inc_own = acts[0], incoming[0]
    got = lax.all_to_all(pack(proj_in, proj_out, valid_rows), "u", 0, 0)
    inc_par = lax.ppermute(inc_own, "c", swap)
    act_par = lax.ppermute(act_own, "c", swap)
    sent, valid = split(got)
    w = lax.all_to_all(sent, ("y", "p"), 0, 0).reshape(NY, NP, NU, 64, 128)
    came = [valid] + [
        lax.ppermute(valid, "y", [(i, (i + k) % NY) for i in range(NY)]) for k in range(1, NY)
    ]
    sums = project_grads(w, inc_own, inc_par)
    sums, came = lax.optimization_barrier((sums, came))
    parts = lax.all_to_all(sums, ("x", "c"), 0, 0)
    here = merge(came)
    there = lax.ppermute(here, "p", swap)
    mine, others = project_acts(w, act_own, act_par)
    theirs = lax.ppermute(others, "c", swap)
    scores = score(lengths, parts, mine, theirs, here, there)
    scores = lax.all_to_all(scores.reshape(64, 1, 128), ("y", "u", "p"), 0, 0).reshape(64, 128)
    return gram(domains.reshape(1, 64), scores)[None, None]


def solution(mesh):
    fine = Mesh(mesh.devices.reshape(SIZES), AXES)
    pipe, dp = AXES[:2], AXES[2:]
    placed = (
        P(pipe, dp, None),
        P(pipe, dp, None),
        P(None, dp),
        P(None, dp),
        P(pipe, dp, None),
        P(dp),
        P(),
    )
    return jax.shard_map(
        body, mesh=fine, in_specs=placed, out_specs=P(pipe, dp, None, None), check_vma=False
    )
```

time: 105 us -> 103 us (0.981)
  blocking collectives: 27.4 us -> 55.9 us
  starting transfers between devices: 45.4 us -> 29.7 us
  waiting for transfers between devices: 17 us -> 2.3 us
    all_to_all x1 -> x2, blocking collectives: 27.4 us -> 55.9 us  [the longest x1 36.5 us: body(): got = lax.all_to_all(pack(proj_in, proj_out, valid_rows), 'u', 0, 0)]
    all_to_all x3 -> x2, starting transfers between devices: 27.7 us -> 9.31 us  [the longest x1 4.84 us: body(): parts = lax.all_to_all(sums, ('x', 'c'), 0, 0)]
    all_to_all x3 -> x2, waiting for transfers between devices: 16.4 us -> 0.01 us  [the longest x1 0.01 us: body(): parts = lax.all_to_all(sums, ('x', 'c'), 0, 0)]
    ppermute x3 -> x4, starting transfers between devices: 11.3 us -> 14 us  [the longest x3 10.7 us: body(): lax.ppermute(valid, 'y', [(i, (i + k) % NY) for i in range(NY)])]
    ppermute x3 -> x4, waiting for transfers between devices: 0.01 us -> 1.71 us  [the longest x3 1.71 us: body(): lax.ppermute(valid, 'y', [(i, (i + k) % NY) for i in range(NY)])]
    pallas_call x2 -> x3, Pallas kernels: 2.72 us -> 2.63 us  [the longest x1 1.49 us: pack(): pl.pallas_call(pack_kernel, out_shape=pltpu.HBM((NU, 128, 128), bf16), in...]
  transfers between devices with their start and end apart: 9 -> 9, of which waited for: 2 -> 2; matrix products, arithmetic and copies ran while one was open for 0% -> 0% of each run, Pallas kernels for 9% -> 8%
where the time goes in v3:
time: 103 us; the launch traced here: 102 us
  blocking collectives  55.9 us (54%)
  starting transfers between devices  29.7 us (29%)
  Pallas kernels  13.6 us (13%)
  waiting for transfers between devices  2.3 us (2%)
    all_to_all x1, blocking collectives, body(): got = lax.all_to_all(pack(proj_in, proj_out, valid_rows), 'u', 0, 0)  36.5 us
    all_to_all x1, blocking collectives, body(): lax.all_to_all(scores.reshape(64, 1, 128), ('y', 'u', 'p'), 0, 0)  19.4 us
    ppermute x3, starting transfers between devices, body(): lax.ppermute(valid, 'y', [(i, (i + k) % NY) for i in range(NY)])  10.7 us
    all_to_all x1, starting transfers between devices, body(): parts = lax.all_to_all(sums, ('x', 'c'), 0, 0)  4.84 us
    all_to_all x1, starting transfers between devices, body(): w = lax.all_to_all(sent, ('y', 'p'), 0, 0).reshape(NY, NP, NU, 64, 128)  4.47 us
    pallas_call x1, Pallas kernels, project_grads(): pl.pallas_call(grad_kernel, out_shape=pltpu.HBM((NX * NC, 32, 128), f32),...  4.2 us
    pallas_call x1, Pallas kernels, project_acts(): pl.pallas_call(act_kernel, out_shape=(jax.ShapeDtypeStruct((32, 128), f32...  4.16 us
    ppermute x1, starting transfers between devices, body(): there = lax.ppermute(here, 'p', swap)  3.37 us
  transfers between devices with their start and end apart: 9, of which 2 were waited for; matrix products, arithmetic and copies ran while one was open for 0% of the time, Pallas kernels for 8%

profile of v3, /device:TPU:2, one launch (start us, length us, event | category | flops | bytes accessed | tf_op | source)
XLA Modules:
  0.0 102.3 jit_solution(10754382607989346599)
XLA Ops:
  0.0 1.5 %shard_map.73 = bf16[8,128,128]{2,1,0:T(8,128)(2,1)} custom-call(bf16[64,128]{1,0:T(8,128)(2,1)} %in_ref.1, bf16[64,128]{1,0:T(8,128)(2,1)} %out_ref.1, bf16[1,2,4096]{2,1,0:T(2,128)(2,1)} %valid_ref.1), custom_call_target="tpu_custom_call" | custom-call | bytes 311296 | tf_op jit(solution)/shard_map/pallas_call | solution.py:46
  1.5 36.5 %all_to_all.20.got_ref = bf16[8,128,128]{2,1,0:T(8,128)(2,1)S(1)} all-to-all(bf16[8,128,128]{2,1,0:T(8,128)(2,1)} %shard_map.73), channel_id=1, replica_groups=mesh['x'=4,'c'=2,'y'=4,'u'=8,'p'=2] {'u'}, dimensions={0} | all-to-all | bytes 524288 | tf_op jit(solution)/shard_map/all_to_all | solution.py:241
  37.9 1.1 %shard_map.74 = (bf16[8,8,64,128]{3,2,1,0:T(8,128)(2,1)}, bf16[8,64,128]{2,1,0:T(8,128)(2,1)S(1)}) custom-call(bf16[8,128,128]{2,1,0:T(8,128)(2,1)S(1)} %all_to_all.20.got_ref), custom_call_target="tpu_custom_call" | custom-call | bytes 1572864 | tf_op jit(solution)/shard_map/pallas_call | solution.py:63
  39.1 4.5 %all-to-all-start.1 = ((bf16[8,8,64,128]{3,2,1,0:T(8,128)(2,1)}), bf16[8,8,64,128]{3,2,1,0:T(8,128)(2,1)S(1)}, u32[]{:S(2)}, u32[]{:S(2)}) async-start(bf16[8,8,64,128]{3,2,1,0:T(8,128)(2,1)} %get-tuple-element.14), calls=%async_computation.1 | async-start | bytes 2097152 | tf_op jit(solution)/shard_map/all_to_all | solution.py:245
  43.5 1.9 %collective-permute-start = (bf16[128,8192]{1,0:T(8,128)(2,1)}, bf16[128,8192]{1,0:T(8,128)(2,1)}, u32[]{:S(2)}, u32[]{:S(2)}) collective-permute-start(bf16[128,8192]{1,0:T(8,128)(2,1)} %bitcast.2.own_ref), channel_id=1, source_target_pairs={{0,64},{64,0},{1,65},{65,1},{2,66},{66,2},{3,67},{67,3},{4,68},{68... | collective-permute-start | bytes 6291464 | tf_op jit(solution)/shard_map/ppermute | solution.py:242
  45.4 2.4 %collective-permute-start.4 = (bf16[128,8192]{1,0:T(8,128)(2,1)}, bf16[128,8192]{1,0:T(8,128)(2,1)}, u32[]{:S(2)}, u32[]{:S(2)}) collective-permute-start(bf16[128,8192]{1,0:T(8,128)(2,1)} %bitcast.3.own_ref), channel_id=1, source_target_pairs={{0,64},{64,0},{1,65},{65,1},{2,66},{66,2},{3,67},{67,3},{4,68},{68... | collective-permute-start | bytes 6291464 | tf_op jit(solution)/shard_map/ppermute | solution.py:243
  47.9 5.1 %collective-permute-start.3 = (bf16[8,64,128]{2,1,0:T(8,128)(2,1)S(1)}, bf16[8,64,128]{2,1,0:T(8,128)(2,1)S(1)}, u32[]{:S(2)}, u32[]{:S(2)}) collective-permute-start(bf16[8,64,128]{2,1,0:T(8,128)(2,1)S(1)} %get-tuple-element.19.refs_0_), channel_id=1, source_target_pairs={{0,48},{16,0},{32,16},{48,32},{1,49},{17,1},{33,17},{49,33},{2,50}... | collective-permute-start | bytes 393224 | tf_op jit(solution)/shard_map/ppermute | solution.py:247
  53.0 2.8 %collective-permute-start.2 = (bf16[8,64,128]{2,1,0:T(8,128)(2,1)S(1)}, bf16[8,64,128]{2,1,0:T(8,128)(2,1)S(1)}, u32[]{:S(2)}, u32[]{:S(2)}) collective-permute-start(bf16[8,64,128]{2,1,0:T(8,128)(2,1)S(1)} %get-tuple-element.19.refs_0_), channel_id=1, source_target_pairs={{0,32},{16,48},{32,0},{48,16},{1,33},{17,49},{33,1},{49,17},{2,34}... | collective-permute-start | bytes 393224 | tf_op jit(solution)/shard_map/ppermute | solution.py:247
  55.8 2.8 %collective-permute-start.1 = (bf16[8,64,128]{2,1,0:T(8,128)(2,1)S(1)}, bf16[8,64,128]{2,1,0:T(8,128)(2,1)S(1)}, u32[]{:S(2)}, u32[]{:S(2)}) collective-permute-start(bf16[8,64,128]{2,1,0:T(8,128)(2,1)S(1)} %get-tuple-element.19.refs_0_), channel_id=1, source_target_pairs={{0,16},{16,32},{32,48},{48,0},{1,17},{17,33},{33,49},{49,1},{2,18}... | collective-permute-start | bytes 393224 | tf_op jit(solution)/shard_map/ppermute | solution.py:247
  58.6 0.0 collective-permute-done.par_ref
  58.6 0.0 all-to-all-done.1
  58.6 4.2 %shard_map.75 = f32[8,32,128]{2,1,0:T(8,128)} custom-call(bf16[4,2,8,64,128]{4,3,2,1,0:T(8,128)(2,1)S(1)} %bitcast.9, bf16[128,8192]{1,0:T(8,128)(2,1)} %bitcast.2.own_ref, bf16[128,8192]{1,0:T(8,128)(2,1)} %collective-permute-done.par_ref), custom_call_target="tpu_custom_call" | custom-call | flops 268435456 | bytes 5242880 | tf_op jit(solution)/shard_map/pallas_call | solution.py:144
  62.8 0.0 collective-permute-done.3.refs_3_
  62.8 0.0 collective-permute-done.2.refs_2_
  62.8 1.7 %collective-permute-done.1.refs_1_ = bf16[8,64,128]{2,1,0:T(8,128)(2,1)S(1)} collective-permute-done((bf16[8,64,128]{2,1,0:T(8,128)(2,1)S(1)}, bf16[8,64,128]{2,1,0:T(8,128)(2,1)S(1)}, u32[]{:S(2)}, u32[]{:S(2)}) %collective-permute-start.1) | collective-permute-done | bytes 131104 | tf_op jit(solution)/shard_map/ppermute | solution.py:247
  64.5 3.4 %collective-permute-start.6 = (bf16[4,8,64,128]{3,2,1,0:T(8,128)(2,1)S(1)}, bf16[4,8,64,128]{3,2,1,0:T(8,128)(2,1)S(1)}, u32[]{:S(2)}, u32[]{:S(2)}) collective-permute-start(bf16[4,8,64,128]{3,2,1,0:T(8,128)(2,1)S(1)} %shard_map.77.here_ref), channel_id=1, source_target_pairs={{0,1},{1,0},{2,3},{3,2},{4,5},{5,4},{6,7},{7,6},{8,9},{9,8},{10,11... | collective-permute-start | bytes 1572872 | tf_op jit(solution)/shard_map/ppermute | solution.py:253
  67.9 4.8 %all-to-all-start.2 = ((f32[8,32,128]{2,1,0:T(8,128)}), f32[8,32,128]{2,1,0:T(8,128)S(1)}, u32[]{:S(2)}, u32[]{:S(2)}) async-start(f32[8,32,128]{2,1,0:T(8,128)} %shard_map.75), calls=%async_computation.2 | async-start | bytes 262144 | tf_op jit(solution)/shard_map/all_to_all | solution.py:251
  72.8 0.0 copy-start
  72.8 0.0 collective-permute-done.4.par_ref
  72.8 4.2 %shard_map.76 = (f32[32,128]{1,0:T(8,128)S(1)}, f32[32,128]{1,0:T(8,128)}) custom-call(bf16[4,2,8,64,128]{4,3,2,1,0:T(8,128)(2,1)S(1)} %bitcast.10, bf16[128,8192]{1,0:T(8,128)(2,1)} %bitcast.3.own_ref, bf16[128,8192]{1,0:T(8,128)(2,1)} %collective-permute-done.4.par_ref), custom_call_target="tpu_custom_call" | custom-call | flops 268435456 | bytes 5242880 | tf_op jit(solution)/shard_map/pallas_call | solution.py:156
  76.9 2.1 %collective-permute-start.5 = (f32[32,128]{1,0:T(8,128)}, f32[32,128]{1,0:T(8,128)S(1)}, u32[]{:S(2)}, u32[]{:S(2)}) collective-permute-start(f32[32,128]{1,0:T(8,128)} %get-tuple-element.18), channel_id=1, source_target_pairs={{0,64},{64,0},{1,65},{65,1},{2,66},{66,2},{3,67},{67,3},{4,68},{68... | collective-permute-start | bytes 49160 | tf_op jit(solution)/shard_map/ppermute | solution.py:255
  79.7 0.6 collective-permute-done.5.theirs_ref
  80.2 0.0 all-to-all-done.2.parts_ref
  80.2 0.0 collective-permute-done.6.there_ref
  80.2 1.7 %shard_map.78 = f32[64,128]{1,0:T(8,128)} custom-call(s32[1]{0:T(128)S(6)} %copy.9.len_ref, f32[8,32,128]{2,1,0:T(8,128)S(1)} %all-to-all-done.2.parts_ref, f32[32,128]{1,0:T(8,128)S(1)} %get-tuple-element.17.mine_ref, f32[32,128]{1,0:T(8,128)S(1)} %collective-permute-done.5.theirs_ref, bf16[4,8,64,128]{3,2,1,0:T(8,128)(2,1)S(1)} %shard_map.77.here_ref, ...), custom_call_target="tpu_custom_call" | custom-call | flops 1048576 | bytes 1048576 | tf_op jit(solution)/shard_map/pallas_call | solution.py:208
  82.0 19.4 %all_to_all.21 = f32[64,1,128]{2,1,0:T(1,128)S(1)} all-to-all(f32[64,1,128]{2,1,0:T(1,128)} %bitcast.13), channel_id=1, replica_groups=mesh['x'=4,'c'=2,'y'=4,'u'=8,'p'=2] {'y','u','p'}, dimensions={0} | all-to-all | bytes 65536 | tf_op jit(solution)/shard_map/all_to_all | solution.py:257
  101.4 0.0 copy-done
  101.4 0.9 shard_map.79
  (1 shorter events, 0.0 us)
Async XLA Ops:
  39.1 19.5 %all-to-all-start.1 = ((bf16[8,8,64,128]{3,2,1,0:T(8,128)(2,1)}), bf16[8,8,64,128]{3,2,1,0:T(8,128)(2,1)S(1)}, u32[]{:S(2)}, u32[]{:S(2)}) async-start(bf16[8,8,64,128]{3,2,1,0:T(8,128)(2,1)} %get-tuple-element.14), calls=%async_computation.1 | async-start | bytes 2097152 | tf_op jit(solution)/shard_map/all_to_all | solution.py:245
  43.5 15.0 %collective-permute-start = (bf16[128,8192]{1,0:T(8,128)(2,1)}, bf16[128,8192]{1,0:T(8,128)(2,1)}, u32[]{:S(2)}, u32[]{:S(2)}) collective-permute-start(bf16[128,8192]{1,0:T(8,128)(2,1)} %bitcast.2.own_ref), channel_id=1, source_target_pairs={{0,64},{64,0},{1,65},{65,1},{2,66},{66,2},{3,67},{67,3},{4,68},{68... | collective-permute-start | bytes 6291464 | tf_op jit(solution)/shard_map/ppermute | solution.py:242
  45.4 27.3 %collective-permute-start.4 = (bf16[128,8192]{1,0:T(8,128)(2,1)}, bf16[128,8192]{1,0:T(8,128)(2,1)}, u32[]{:S(2)}, u32[]{:S(2)}) collective-permute-start(bf16[128,8192]{1,0:T(8,128)(2,1)} %bitcast.3.own_ref), channel_id=1, source_target_pairs={{0,64},{64,0},{1,65},{65,1},{2,66},{66,2},{3,67},{67,3},{4,68},{68... | collective-permute-start | bytes 6291464 | tf_op jit(solution)/shard_map/ppermute | solution.py:243
  47.9 14.9 %collective-permute-start.3 = (bf16[8,64,128]{2,1,0:T(8,128)(2,1)S(1)}, bf16[8,64,128]{2,1,0:T(8,128)(2,1)S(1)}, u32[]{:S(2)}, u32[]{:S(2)}) collective-permute-start(bf16[8,64,128]{2,1,0:T(8,128)(2,1)S(1)} %get-tuple-element.19.refs_0_), channel_id=1, source_target_pairs={{0,48},{16,0},{32,16},{48,32},{1,49},{17,1},{33,17},{49,33},{2,50}... | collective-permute-start | bytes 393224 | tf_op jit(solution)/shard_map/ppermute | solution.py:247
  53.0 9.8 %collective-permute-start.2 = (bf16[8,64,128]{2,1,0:T(8,128)(2,1)S(1)}, bf16[8,64,128]{2,1,0:T(8,128)(2,1)S(1)}, u32[]{:S(2)}, u32[]{:S(2)}) collective-permute-start(bf16[8,64,128]{2,1,0:T(8,128)(2,1)S(1)} %get-tuple-element.19.refs_0_), channel_id=1, source_target_pairs={{0,32},{16,48},{32,0},{48,16},{1,33},{17,49},{33,1},{49,17},{2,34}... | collective-permute-start | bytes 393224 | tf_op jit(solution)/shard_map/ppermute | solution.py:247
  55.8 8.7 %collective-permute-start.1 = (bf16[8,64,128]{2,1,0:T(8,128)(2,1)S(1)}, bf16[8,64,128]{2,1,0:T(8,128)(2,1)S(1)}, u32[]{:S(2)}, u32[]{:S(2)}) collective-permute-start(bf16[8,64,128]{2,1,0:T(8,128)(2,1)S(1)} %get-tuple-element.19.refs_0_), channel_id=1, source_target_pairs={{0,16},{16,32},{32,48},{48,0},{1,17},{17,33},{33,49},{49,1},{2,18}... | collective-permute-start | bytes 393224 | tf_op jit(solution)/shard_map/ppermute | solution.py:247
  64.5 15.7 %collective-permute-start.6 = (bf16[4,8,64,128]{3,2,1,0:T(8,128)(2,1)S(1)}, bf16[4,8,64,128]{3,2,1,0:T(8,128)(2,1)S(1)}, u32[]{:S(2)}, u32[]{:S(2)}) collective-permute-start(bf16[4,8,64,128]{3,2,1,0:T(8,128)(2,1)S(1)} %shard_map.77.here_ref), channel_id=1, source_target_pairs={{0,1},{1,0},{2,3},{3,2},{4,5},{5,4},{6,7},{7,6},{8,9},{9,8},{10,11... | collective-permute-start | bytes 1572872 | tf_op jit(solution)/shard_map/ppermute | solution.py:253
  67.9 12.3 %all-to-all-start.2 = ((f32[8,32,128]{2,1,0:T(8,128)}), f32[8,32,128]{2,1,0:T(8,128)S(1)}, u32[]{:S(2)}, u32[]{:S(2)}) async-start(f32[8,32,128]{2,1,0:T(8,128)} %shard_map.75), calls=%async_computation.2 | async-start | bytes 262144 | tf_op jit(solution)/shard_map/all_to_all | solution.py:251
  72.8 28.6 %copy-start = (s32[64]{0:T(128)S(1)}, s32[64]{0:T(128)}, u32[]{:S(2)}) copy-start(s32[64]{0:T(128)} %param.13) | copy-start | bytes 772
  76.9 3.3 %collective-permute-start.5 = (f32[32,128]{1,0:T(8,128)}, f32[32,128]{1,0:T(8,128)S(1)}, u32[]{:S(2)}, u32[]{:S(2)}) collective-permute-start(f32[32,128]{1,0:T(8,128)} %get-tuple-element.18), channel_id=1, source_target_pairs={{0,64},{64,0},{1,65},{65,1},{2,66},{66,2},{3,67},{67,3},{4,68},{68... | collective-permute-start | bytes 49160 | tf_op jit(solution)/shard_map/ppermute | solution.py:255

commit v4 on v3

--- a/solution.py
+++ b/solution.py
@@ -30,40 +30,40 @@
 
 
 def pack_kernel(in_ref, out_ref, valid_ref, sent_ref, proj_ref, rows_ref):
-    c = lax.axis_index("c")
+    x, c = lax.axis_index("x"), lax.axis_index("c")
     proj_ref[0] = in_ref[...].astype(f32)
     proj_ref[1] = out_ref[...].astype(f32)
-    rows_ref[0:32] = proj_ref[0, pl.ds(pl.multiple_of(c * 32, 32), 32)]
-    rows_ref[32:64] = proj_ref[1, pl.ds(c, 32, stride=2)]
+    rows_ref[0:8] = proj_ref[0, pl.ds(c * 32 + x * 8, 8)]
+    rows_ref[8:16] = proj_ref[1, pl.ds(x * 16 + c, 8, stride=2)]
     for r in range(32):
         pair = valid_ref[0, :, r * 128 : (r + 1) * 128].astype(f32)
-        rows_ref[64 + r : 65 + r] = pair[0:1]
-        rows_ref[96 + r : 97 + r] = pair[1:2]
-    sent_ref[...] = jnp.broadcast_to(rows_ref[...].astype(bf16)[None], (NU, 128, 128))
+        rows_ref[16 + r : 17 + r] = pair[0:1]
+        rows_ref[48 + r : 49 + r] = pair[1:2]
+    sent_ref[...] = jnp.broadcast_to(rows_ref[...].astype(bf16)[None], (NU, 80, 128))
 
 
 def pack(proj_in, proj_out, valid_rows):
     return pl.pallas_call(
         pack_kernel,
-        out_shape=pltpu.HBM((NU, 128, 128), bf16),
+        out_shape=pltpu.HBM((NU, 80, 128), bf16),
         in_specs=[VMEM] * 3,
         out_specs=VMEM,
-        scratch_shapes=[pltpu.VMEM((2, 64, 128), f32), pltpu.VMEM((128, 128), f32)],
-        compiler_params=params(32),
-        cost_estimate=cost(0, 304 * 1024),
+        scratch_shapes=[pltpu.VMEM((2, 64, 128), f32), pltpu.VMEM((80, 128), f32)],
+        compiler_params=params(32),
+        cost_estimate=cost(0, 208 * 1024),
     )(*in_hbm(proj_in, proj_out, valid_rows))
 
 
 def split_kernel(got_ref, proj_ref, valid_ref):
-    proj_ref[...] = jnp.broadcast_to(got_ref[:, 0:64][None], (NY * NP, NU, 64, 128))
-    valid_ref[...] = got_ref[:, 64:128]
+    proj_ref[...] = jnp.broadcast_to(got_ref[:, 0:16][None], (NX * NY * NP, NU, 16, 128))
+    valid_ref[...] = got_ref[:, 16:80]
 
 
 def split(got):
     return pl.pallas_call(
         split_kernel,
         out_shape=(
-            pltpu.HBM((NY * NP, NU, 64, 128), bf16),
+            pltpu.HBM((NX * NY * NP, NU, 16, 128), bf16),
             jax.ShapeDtypeStruct((NU, 64, 128), bf16),
         ),
         in_specs=[VMEM],
@@ -105,7 +105,7 @@
     for half in range(2):
         w = jnp.concatenate(
             [
-                w_ref[y, p, u, which * 32 : which * 32 + 32]
+                w_ref[:, y, p, u].reshape(NX * 16, 128)
                 for y in range(2 * half, 2 * half + 2)
                 for u in range(NU)
                 for p in range(NP)
@@ -118,6 +118,7 @@
             w, data_ref[:, half * wide : (half + 1) * wide], NT, preferred_element_type=f32
         )
         total = part if total is None else total + part
+    total = total.reshape(NX, 2, 8, 256)[:, which].reshape(32, 256)
     return total[:, 0:128], total[:, 128:256]
 
 
@@ -242,7 +243,7 @@
     inc_par = lax.ppermute(inc_own, "c", swap)
     act_par = lax.ppermute(act_own, "c", swap)
     sent, valid = split(got)
-    w = lax.all_to_all(sent, ("y", "p"), 0, 0).reshape(NY, NP, NU, 64, 128)
+    w = lax.all_to_all(sent, ("x", "y", "p"), 0, 0).reshape(NX, NY, NP, NU, 16, 128)
     came = [valid] + [
         lax.ppermute(valid, "y", [(i, (i + k) % NY) for i in range(NY)]) for k in range(1, NY)
     ]

time: 103 us -> 102 us (level)
  the two profiles are of different devices: /device:TPU:2 before, /device:TPU:8 now
where the time goes in v4:
time: 102 us; the launch traced here: 101 us
  blocking collectives  54.1 us (53%)
  starting transfers between devices  32.4 us (32%)
  Pallas kernels  13.7 us (13%)
    all_to_all x1, blocking collectives, body(): got = lax.all_to_all(pack(proj_in, proj_out, valid_rows), 'u', 0, 0)  32.4 us
    all_to_all x1, blocking collectives, body(): lax.all_to_all(scores.reshape(64, 1, 128), ('y', 'u', 'p'), 0, 0)  21.7 us
    ppermute x3, starting transfers between devices, body(): lax.ppermute(valid, 'y', [(i, (i + k) % NY) for i in range(NY)])  10.4 us
    all_to_all x1, starting transfers between devices, body(): lax.all_to_all(sent, ('x', 'y', 'p'), 0, 0).reshape(NX, NY, NP, NU, 16, 128)  7.53 us
    all_to_all x1, starting transfers between devices, body(): parts = lax.all_to_all(sums, ('x', 'c'), 0, 0)  4.29 us
    pallas_call x1, Pallas kernels, project_grads(): pl.pallas_call(grad_kernel, out_shape=pltpu.HBM((NX * NC, 32, 128), f32),...  4.23 us
    pallas_call x1, Pallas kernels, project_acts(): pl.pallas_call(act_kernel, out_shape=(jax.ShapeDtypeStruct((32, 128), f32...  4.19 us
    ppermute x1, starting transfers between devices, body(): there = lax.ppermute(here, 'p', swap)  3.38 us
  transfers between devices with their start and end apart: 9, of which 1 were waited for; matrix products, arithmetic and copies ran while one was open for 0% of the time, Pallas kernels for 8%

profile of v4, /device:TPU:8, one launch (start us, length us, event | category | flops | bytes accessed | tf_op | source)
XLA Modules:
  0.0 101.4 jit_solution(12968430995093044184)
XLA Ops:
  0.0 1.5 %shard_map.73 = bf16[8,80,128]{2,1,0:T(8,128)(2,1)} custom-call(bf16[64,128]{1,0:T(8,128)(2,1)} %in_ref.1, bf16[64,128]{1,0:T(8,128)(2,1)} %out_ref.1, bf16[1,2,4096]{2,1,0:T(2,128)(2,1)} %valid_ref.1), custom_call_target="tpu_custom_call" | custom-call | bytes 212992 | tf_op jit(solution)/shard_map/pallas_call | solution.py:46
  1.5 32.4 %all_to_all.20.got_ref = bf16[8,80,128]{2,1,0:T(8,128)(2,1)S(1)} all-to-all(bf16[8,80,128]{2,1,0:T(8,128)(2,1)} %shard_map.73), channel_id=1, replica_groups=mesh['x'=4,'c'=2,'y'=4,'u'=8,'p'=2] {'u'}, dimensions={0} | all-to-all | bytes 327680 | tf_op jit(solution)/shard_map/all_to_all | solution.py:242
  33.8 1.2 %shard_map.74 = (bf16[32,8,16,128]{3,2,1,0:T(8,128)(2,1)}, bf16[8,64,128]{2,1,0:T(8,128)(2,1)S(1)}) custom-call(bf16[8,80,128]{2,1,0:T(8,128)(2,1)S(1)} %all_to_all.20.got_ref), custom_call_target="tpu_custom_call" | custom-call | bytes 1572864 | tf_op jit(solution)/shard_map/pallas_call | solution.py:63
  35.0 7.5 %all-to-all-start.1 = ((bf16[32,8,16,128]{3,2,1,0:T(8,128)(2,1)}), bf16[32,8,16,128]{3,2,1,0:T(8,128)(2,1)S(1)}, u32[]{:S(2)}, u32[]{:S(2)}) async-start(bf16[32,8,16,128]{3,2,1,0:T(8,128)(2,1)} %get-tuple-element.14), calls=%async_computation.1 | async-start | bytes 2097152 | tf_op jit(solution)/shard_map/all_to_all | solution.py:246
  42.6 1.9 %collective-permute-start = (bf16[128,8192]{1,0:T(8,128)(2,1)}, bf16[128,8192]{1,0:T(8,128)(2,1)}, u32[]{:S(2)}, u32[]{:S(2)}) collective-permute-start(bf16[128,8192]{1,0:T(8,128)(2,1)} %bitcast.2.own_ref), channel_id=1, source_target_pairs={{0,64},{64,0},{1,65},{65,1},{2,66},{66,2},{3,67},{67,3},{4,68},{68... | collective-permute-start | bytes 6291464 | tf_op jit(solution)/shard_map/ppermute | solution.py:243
  44.5 2.4 %collective-permute-start.4 = (bf16[128,8192]{1,0:T(8,128)(2,1)}, bf16[128,8192]{1,0:T(8,128)(2,1)}, u32[]{:S(2)}, u32[]{:S(2)}) collective-permute-start(bf16[128,8192]{1,0:T(8,128)(2,1)} %bitcast.3.own_ref), channel_id=1, source_target_pairs={{0,64},{64,0},{1,65},{65,1},{2,66},{66,2},{3,67},{67,3},{4,68},{68... | collective-permute-start | bytes 6291464 | tf_op jit(solution)/shard_map/ppermute | solution.py:244
  46.9 2.1 %collective-permute-start.3 = (bf16[8,64,128]{2,1,0:T(8,128)(2,1)S(1)}, bf16[8,64,128]{2,1,0:T(8,128)(2,1)S(1)}, u32[]{:S(2)}, u32[]{:S(2)}) collective-permute-start(bf16[8,64,128]{2,1,0:T(8,128)(2,1)S(1)} %get-tuple-element.19.refs_0_), channel_id=1, source_target_pairs={{0,48},{16,0},{32,16},{48,32},{1,49},{17,1},{33,17},{49,33},{2,50}... | collective-permute-start | bytes 393224 | tf_op jit(solution)/shard_map/ppermute | solution.py:248
  49.1 4.6 %collective-permute-start.2 = (bf16[8,64,128]{2,1,0:T(8,128)(2,1)S(1)}, bf16[8,64,128]{2,1,0:T(8,128)(2,1)S(1)}, u32[]{:S(2)}, u32[]{:S(2)}) collective-permute-start(bf16[8,64,128]{2,1,0:T(8,128)(2,1)S(1)} %get-tuple-element.19.refs_0_), channel_id=1, source_target_pairs={{0,32},{16,48},{32,0},{48,16},{1,33},{17,49},{33,1},{49,17},{2,34}... | collective-permute-start | bytes 393224 | tf_op jit(solution)/shard_map/ppermute | solution.py:248
  53.7 3.7 %collective-permute-start.1 = (bf16[8,64,128]{2,1,0:T(8,128)(2,1)S(1)}, bf16[8,64,128]{2,1,0:T(8,128)(2,1)S(1)}, u32[]{:S(2)}, u32[]{:S(2)}) collective-permute-start(bf16[8,64,128]{2,1,0:T(8,128)(2,1)S(1)} %get-tuple-element.19.refs_0_), channel_id=1, source_target_pairs={{0,16},{16,32},{32,48},{48,0},{1,17},{17,33},{33,49},{49,1},{2,18}... | collective-permute-start | bytes 393224 | tf_op jit(solution)/shard_map/ppermute | solution.py:248
  57.4 0.0 collective-permute-done.par_ref
  57.4 0.0 all-to-all-done.1
  57.4 4.2 %shard_map.75 = f32[8,32,128]{2,1,0:T(8,128)} custom-call(bf16[4,4,2,8,16,128]{5,4,3,2,1,0:T(8,128)(2,1)S(1)} %bitcast.9, bf16[128,8192]{1,0:T(8,128)(2,1)} %bitcast.2.own_ref, bf16[128,8192]{1,0:T(8,128)(2,1)} %collective-permute-done.par_ref), custom_call_target="tpu_custom_call" | custom-call | flops 268435456 | bytes 5242880 | tf_op jit(solution)/shard_map/pallas_call | solution.py:145
  61.6 0.0 collective-permute-done.3.refs_3_
  61.6 0.0 collective-permute-done.2.refs_2_
  61.7 0.0 collective-permute-done.1.refs_1_
  61.7 3.4 %collective-permute-start.6 = (bf16[4,8,64,128]{3,2,1,0:T(8,128)(2,1)S(1)}, bf16[4,8,64,128]{3,2,1,0:T(8,128)(2,1)S(1)}, u32[]{:S(2)}, u32[]{:S(2)}) collective-permute-start(bf16[4,8,64,128]{3,2,1,0:T(8,128)(2,1)S(1)} %shard_map.77.here_ref), channel_id=1, source_target_pairs={{0,1},{1,0},{2,3},{3,2},{4,5},{5,4},{6,7},{7,6},{8,9},{9,8},{10,11... | collective-permute-start | bytes 1572872 | tf_op jit(solution)/shard_map/ppermute | solution.py:254
  65.1 4.3 %all-to-all-start.2 = ((f32[8,32,128]{2,1,0:T(8,128)}), f32[8,32,128]{2,1,0:T(8,128)S(1)}, u32[]{:S(2)}, u32[]{:S(2)}) async-start(f32[8,32,128]{2,1,0:T(8,128)} %shard_map.75), calls=%async_computation.2 | async-start | bytes 262144 | tf_op jit(solution)/shard_map/all_to_all | solution.py:252
  69.4 0.0 copy-start
  69.4 0.0 collective-permute-done.4.par_ref
  69.4 4.2 %shard_map.76 = (f32[32,128]{1,0:T(8,128)S(1)}, f32[32,128]{1,0:T(8,128)}) custom-call(bf16[4,4,2,8,16,128]{5,4,3,2,1,0:T(8,128)(2,1)S(1)} %bitcast.10, bf16[128,8192]{1,0:T(8,128)(2,1)} %bitcast.3.own_ref, bf16[128,8192]{1,0:T(8,128)(2,1)} %collective-permute-done.4.par_ref), custom_call_target="tpu_custom_call" | custom-call | flops 268435456 | bytes 5242880 | tf_op jit(solution)/shard_map/pallas_call | solution.py:157
  73.6 2.4 %collective-permute-start.5 = (f32[32,128]{1,0:T(8,128)}, f32[32,128]{1,0:T(8,128)S(1)}, u32[]{:S(2)}, u32[]{:S(2)}) collective-permute-start(f32[32,128]{1,0:T(8,128)} %get-tuple-element.18), channel_id=1, source_target_pairs={{0,64},{64,0},{1,65},{65,1},{2,66},{66,2},{3,67},{67,3},{4,68},{68... | collective-permute-start | bytes 49160 | tf_op jit(solution)/shard_map/ppermute | solution.py:256
  76.7 0.4 collective-permute-done.5.theirs_ref
  77.0 0.0 all-to-all-done.2.parts_ref
  77.0 0.0 collective-permute-done.6.there_ref
  77.0 1.7 %shard_map.78 = f32[64,128]{1,0:T(8,128)} custom-call(s32[1]{0:T(128)S(6)} %copy.9.len_ref, f32[8,32,128]{2,1,0:T(8,128)S(1)} %all-to-all-done.2.parts_ref, f32[32,128]{1,0:T(8,128)S(1)} %get-tuple-element.17.mine_ref, f32[32,128]{1,0:T(8,128)S(1)} %collective-permute-done.5.theirs_ref, bf16[4,8,64,128]{3,2,1,0:T(8,128)(2,1)S(1)} %shard_map.77.here_ref, ...), custom_call_target="tpu_custom_call" | custom-call | flops 1048576 | bytes 1048576 | tf_op jit(solution)/shard_map/pallas_call | solution.py:209
  78.8 21.7 %all_to_all.21 = f32[64,1,128]{2,1,0:T(1,128)S(1)} all-to-all(f32[64,1,128]{2,1,0:T(1,128)} %bitcast.13), channel_id=1, replica_groups=mesh['x'=4,'c'=2,'y'=4,'u'=8,'p'=2] {'y','u','p'}, dimensions={0} | all-to-all | bytes 65536 | tf_op jit(solution)/shard_map/all_to_all | solution.py:258
  100.5 0.0 copy-done
  100.5 0.9 shard_map.79
  (1 shorter events, 0.0 us)
Async XLA Ops:
  35.0 22.4 %all-to-all-start.1 = ((bf16[32,8,16,128]{3,2,1,0:T(8,128)(2,1)}), bf16[32,8,16,128]{3,2,1,0:T(8,128)(2,1)S(1)}, u32[]{:S(2)}, u32[]{:S(2)}) async-start(bf16[32,8,16,128]{3,2,1,0:T(8,128)(2,1)} %get-tuple-element.14), calls=%async_computation.1 | async-start | bytes 2097152 | tf_op jit(solution)/shard_map/all_to_all | solution.py:246
  42.6 14.8 %collective-permute-start = (bf16[128,8192]{1,0:T(8,128)(2,1)}, bf16[128,8192]{1,0:T(8,128)(2,1)}, u32[]{:S(2)}, u32[]{:S(2)}) collective-permute-start(bf16[128,8192]{1,0:T(8,128)(2,1)} %bitcast.2.own_ref), channel_id=1, source_target_pairs={{0,64},{64,0},{1,65},{65,1},{2,66},{66,2},{3,67},{67,3},{4,68},{68... | collective-permute-start | bytes 6291464 | tf_op jit(solution)/shard_map/ppermute | solution.py:243
  44.5 24.9 %collective-permute-start.4 = (bf16[128,8192]{1,0:T(8,128)(2,1)}, bf16[128,8192]{1,0:T(8,128)(2,1)}, u32[]{:S(2)}, u32[]{:S(2)}) collective-permute-start(bf16[128,8192]{1,0:T(8,128)(2,1)} %bitcast.3.own_ref), channel_id=1, source_target_pairs={{0,64},{64,0},{1,65},{65,1},{2,66},{66,2},{3,67},{67,3},{4,68},{68... | collective-permute-start | bytes 6291464 | tf_op jit(solution)/shard_map/ppermute | solution.py:244
  46.9 14.7 %collective-permute-start.3 = (bf16[8,64,128]{2,1,0:T(8,128)(2,1)S(1)}, bf16[8,64,128]{2,1,0:T(8,128)(2,1)S(1)}, u32[]{:S(2)}, u32[]{:S(2)}) collective-permute-start(bf16[8,64,128]{2,1,0:T(8,128)(2,1)S(1)} %get-tuple-element.19.refs_0_), channel_id=1, source_target_pairs={{0,48},{16,0},{32,16},{48,32},{1,49},{17,1},{33,17},{49,33},{2,50}... | collective-permute-start | bytes 393224 | tf_op jit(solution)/shard_map/ppermute | solution.py:248
  49.1 12.6 %collective-permute-start.2 = (bf16[8,64,128]{2,1,0:T(8,128)(2,1)S(1)}, bf16[8,64,128]{2,1,0:T(8,128)(2,1)S(1)}, u32[]{:S(2)}, u32[]{:S(2)}) collective-permute-start(bf16[8,64,128]{2,1,0:T(8,128)(2,1)S(1)} %get-tuple-element.19.refs_0_), channel_id=1, source_target_pairs={{0,32},{16,48},{32,0},{48,16},{1,33},{17,49},{33,1},{49,17},{2,34}... | collective-permute-start | bytes 393224 | tf_op jit(solution)/shard_map/ppermute | solution.py:248
  53.7 8.0 %collective-permute-start.1 = (bf16[8,64,128]{2,1,0:T(8,128)(2,1)S(1)}, bf16[8,64,128]{2,1,0:T(8,128)(2,1)S(1)}, u32[]{:S(2)}, u32[]{:S(2)}) collective-permute-start(bf16[8,64,128]{2,1,0:T(8,128)(2,1)S(1)} %get-tuple-element.19.refs_0_), channel_id=1, source_target_pairs={{0,16},{16,32},{32,48},{48,0},{1,17},{17,33},{33,49},{49,1},{2,18}... | collective-permute-start | bytes 393224 | tf_op jit(solution)/shard_map/ppermute | solution.py:248
  61.7 15.3 %collective-permute-start.6 = (bf16[4,8,64,128]{3,2,1,0:T(8,128)(2,1)S(1)}, bf16[4,8,64,128]{3,2,1,0:T(8,128)(2,1)S(1)}, u32[]{:S(2)}, u32[]{:S(2)}) collective-permute-start(bf16[4,8,64,128]{3,2,1,0:T(8,128)(2,1)S(1)} %shard_map.77.here_ref), channel_id=1, source_target_pairs={{0,1},{1,0},{2,3},{3,2},{4,5},{5,4},{6,7},{7,6},{8,9},{9,8},{10,11... | collective-permute-start | bytes 1572872 | tf_op jit(solution)/shard_map/ppermute | solution.py:254
  65.1 11.9 %all-to-all-start.2 = ((f32[8,32,128]{2,1,0:T(8,128)}), f32[8,32,128]{2,1,0:T(8,128)S(1)}, u32[]{:S(2)}, u32[]{:S(2)}) async-start(f32[8,32,128]{2,1,0:T(8,128)} %shard_map.75), calls=%async_computation.2 | async-start | bytes 262144 | tf_op jit(solution)/shard_map/all_to_all | solution.py:252
  69.4 31.1 %copy-start = (s32[64]{0:T(128)S(1)}, s32[64]{0:T(128)}, u32[]{:S(2)}) copy-start(s32[64]{0:T(128)} %param.13) | copy-start | bytes 772
  73.6 3.4 %collective-permute-start.5 = (f32[32,128]{1,0:T(8,128)}, f32[32,128]{1,0:T(8,128)S(1)}, u32[]{:S(2)}, u32[]{:S(2)}) collective-permute-start(f32[32,128]{1,0:T(8,128)} %get-tuple-element.18), channel_id=1, source_target_pairs={{0,64},{64,0},{1,65},{65,1},{2,66},{66,2},{3,67},{67,3},{4,68},{68... | collective-permute-start | bytes 49160 | tf_op jit(solution)/shard_map/ppermute | solution.py:256

commit v5 on v4

--- a/solution.py
+++ b/solution.py
@@ -54,23 +54,60 @@
     )(*in_hbm(proj_in, proj_out, valid_rows))
 
 
-def split_kernel(got_ref, proj_ref, valid_ref):
+def stack_kernel(inc_ref, act_ref, both_ref, done_ref, data_ref, in_sems, out_sems):
+    arrive, leave = [], []
+    for j, ref in enumerate((inc_ref, act_ref)):
+        for k in range(2):
+            here, row = pl.ds(k * 64, 64), pl.ds(j * 128 + k * 64, 64)
+            arrive.append(
+                pltpu.make_async_copy(ref.at[here], data_ref.at[row], in_sems.at[j, k])
+            )
+            leave.append(
+                pltpu.make_async_copy(data_ref.at[row], both_ref.at[row], out_sems.at[j, k])
+            )
+    for copy in arrive:
+        copy.start()
+    done_ref[...] = jnp.zeros_like(done_ref)
+    for first, second in zip(arrive, leave):
+        first.wait()
+        second.start()
+    for copy in leave:
+        copy.wait()
+
+
+def stack(inc, act):
+    return pl.pallas_call(
+        stack_kernel,
+        out_shape=(pltpu.HBM((256, 8192), bf16), jax.ShapeDtypeStruct((8, 128), f32)),
+        in_specs=[HBM, HBM],
+        out_specs=(HBM, VMEM),
+        scratch_shapes=[
+            pltpu.VMEM((256, 8192), bf16),
+            pltpu.SemaphoreType.DMA((2, 2)),
+            pltpu.SemaphoreType.DMA((2, 2)),
+        ],
+        compiler_params=params(24),
+        cost_estimate=cost(0, 8 * MIB),
+    )(*in_hbm(inc, act))
+
+
+def split_kernel(got_ref, stacked_ref, proj_ref, valid_ref):
     proj_ref[...] = jnp.broadcast_to(got_ref[:, 0:16][None], (NX * NY * NP, NU, 16, 128))
     valid_ref[...] = got_ref[:, 16:80]
 
 
-def split(got):
+def split(got, stacked):
     return pl.pallas_call(
         split_kernel,
         out_shape=(
             pltpu.HBM((NX * NY * NP, NU, 16, 128), bf16),
             jax.ShapeDtypeStruct((NU, 64, 128), bf16),
         ),
-        in_specs=[VMEM],
+        in_specs=[VMEM, VMEM],
         out_specs=(VMEM, VMEM),
         compiler_params=params(32),
         cost_estimate=cost(0, 1536 * 1024),
-    )(got)
+    )(got, stacked)
 
 
 def merge_kernel(*refs):
@@ -94,8 +131,9 @@
     copies = []
     for half in range(2):
         for k, ref in enumerate((own_ref, par_ref)):
+            first = 0 if k == 0 or which == 1 else 128
             copy = pltpu.make_async_copy(
-                ref.at[:, pl.ds(half * wide, wide)],
+                ref.at[pl.ds(first, 128), pl.ds(half * wide, wide)],
                 data_ref.at[pl.ds(k * 128, 128), pl.ds(half * wide, wide)],
                 sems.at[half, k],
             )
@@ -240,19 +278,19 @@
     swap = [(0, 1), (1, 0)]
     act_own, inc_own = acts[0], incoming[0]
     got = lax.all_to_all(pack(proj_in, proj_out, valid_rows), "u", 0, 0)
-    inc_par = lax.ppermute(inc_own, "c", swap)
-    act_par = lax.ppermute(act_own, "c", swap)
-    sent, valid = split(got)
+    both, stacked = stack(inc_own, act_own)
+    par = lax.ppermute(both, "c", swap)
+    sent, valid = split(got, stacked)
     w = lax.all_to_all(sent, ("x", "y", "p"), 0, 0).reshape(NX, NY, NP, NU, 16, 128)
     came = [valid] + [
         lax.ppermute(valid, "y", [(i, (i + k) % NY) for i in range(NY)]) for k in range(1, NY)
     ]
-    sums = project_grads(w, inc_own, inc_par)
+    sums = project_grads(w, inc_own, par)
     sums, came = lax.optimization_barrier((sums, came))
     parts = lax.all_to_all(sums, ("x", "c"), 0, 0)
     here = merge(came)
     there = lax.ppermute(here, "p", swap)
-    mine, others = project_acts(w, act_own, act_par)
+    mine, others = project_acts(w, act_own, par)
     theirs = lax.ppermute(others, "c", swap)
     scores = score(lengths, parts, mine, theirs, here, there)
     scores = lax.all_to_all(scores.reshape(64, 1, 128), ("y", "u", "p"), 0, 0).reshape(64, 128)

time: 102 us -> 101 us (level)
  the two profiles are of different devices: /device:TPU:8 before, /device:TPU:2 now
where the time goes in v5:
time: 101 us
  starting transfers between devices  45.9 us (45%)
  blocking collectives  21.7 us (21%)
  Pallas kernels  17.1 us (17%)
  waiting for transfers between devices  15.2 us (15%)
    all_to_all x1, blocking collectives, body(): lax.all_to_all(scores.reshape(64, 1, 128), ('y', 'u', 'p'), 0, 0)  21.7 us
    all_to_all x1, starting transfers between devices, body(): got = lax.all_to_all(pack(proj_in, proj_out, valid_rows), 'u', 0, 0)  15.1 us
    all_to_all x1, waiting for transfers between devices, body(): got = lax.all_to_all(pack(proj_in, proj_out, valid_rows), 'u', 0, 0)  12 us
    ppermute x3, starting transfers between devices, body(): lax.ppermute(valid, 'y', [(i, (i + k) % NY) for i in range(NY)])  11.3 us
    all_to_all x1, starting transfers between devices, body(): lax.all_to_all(sent, ('x', 'y', 'p'), 0, 0).reshape(NX, NY, NP, NU, 16, 128)  7.62 us
    all_to_all x1, starting transfers between devices, body(): parts = lax.all_to_all(sums, ('x', 'c'), 0, 0)  4.74 us
    pallas_call x1, Pallas kernels, project_grads(): pl.pallas_call(grad_kernel, out_shape=pltpu.HBM((NX * NC, 32, 128), f32),...  4.24 us
    pallas_call x1, Pallas kernels, project_acts(): pl.pallas_call(act_kernel, out_shape=(jax.ShapeDtypeStruct((32, 128), f32...  4.19 us
  transfers between devices with their start and end apart: 9, of which 4 were waited for; matrix products, arithmetic and copies ran while one was open for 0% of the time, Pallas kernels for 13%

profile of v5, /device:TPU:2, one launch (start us, length us, event | category | flops | bytes accessed | tf_op | source)
XLA Modules:
  0.0 100.8 jit_solution(6645534987684897810)
XLA Ops:
  0.0 1.5 %shard_map.73 = bf16[8,80,128]{2,1,0:T(8,128)(2,1)} custom-call(bf16[64,128]{1,0:T(8,128)(2,1)} %in_ref.1, bf16[64,128]{1,0:T(8,128)(2,1)} %out_ref.1, bf16[1,2,4096]{2,1,0:T(2,128)(2,1)} %valid_ref.1), custom_call_target="tpu_custom_call" | custom-call | bytes 212992 | tf_op jit(solution)/shard_map/pallas_call | solution.py:46
  1.5 15.1 %all-to-all-start = ((bf16[8,80,128]{2,1,0:T(8,128)(2,1)}), bf16[8,80,128]{2,1,0:T(8,128)(2,1)S(1)}, u32[]{:S(2)}, u32[]{:S(2)}) async-start(bf16[8,80,128]{2,1,0:T(8,128)(2,1)} %shard_map.73), calls=%async_computation | async-start | bytes 327680 | tf_op jit(solution)/shard_map/all_to_all | solution.py:280
  16.5 3.3 %shard_map.74 = (bf16[256,8192]{1,0:T(8,128)(2,1)}, f32[8,128]{1,0:T(8,128)S(1)}) custom-call(bf16[128,8192]{1,0:T(8,128)(2,1)} %bitcast.13, bf16[128,8192]{1,0:T(8,128)(2,1)} %bitcast.15), custom_call_target="tpu_custom_call" | custom-call | bytes 8388608 | tf_op jit(solution)/shard_map/pallas_call | solution.py:79
  19.9 1.9 %collective-permute-start = (bf16[256,8192]{1,0:T(8,128)(2,1)}, bf16[256,8192]{1,0:T(8,128)(2,1)}, u32[]{:S(2)}, u32[]{:S(2)}) collective-permute-start(bf16[256,8192]{1,0:T(8,128)(2,1)} %get-tuple-element.18), channel_id=1, source_target_pairs={{0,64},{64,0},{1,65},{65,1},{2,66},{66,2},{3,67},{67,3},{4,68},{68... | collective-permute-start | bytes 12582920 | tf_op jit(solution)/shard_map/ppermute | solution.py:282
  21.8 12.0 %all-to-all-done.got_ref = bf16[8,80,128]{2,1,0:T(8,128)(2,1)S(1)} async-done(((bf16[8,80,128]{2,1,0:T(8,128)(2,1)}), bf16[8,80,128]{2,1,0:T(8,128)(2,1)S(1)}, u32[]{:S(2)}, u32[]{:S(2)}) %all-to-all-start) | async-done | bytes 163872 | tf_op jit(solution)/shard_map/all_to_all | solution.py:280
  33.8 1.3 %shard_map.75 = (bf16[32,8,16,128]{3,2,1,0:T(8,128)(2,1)}, bf16[8,64,128]{2,1,0:T(8,128)(2,1)S(1)}) custom-call(bf16[8,80,128]{2,1,0:T(8,128)(2,1)S(1)} %all-to-all-done.got_ref, f32[8,128]{1,0:T(8,128)S(1)} %get-tuple-element.16.stacked_ref), custom_call_target="tpu_custom_call" | custom-call | bytes 1572864 | tf_op jit(solution)/shard_map/pallas_call | solution.py:100
  35.1 7.6 %all-to-all-start.1 = ((bf16[32,8,16,128]{3,2,1,0:T(8,128)(2,1)}), bf16[32,8,16,128]{3,2,1,0:T(8,128)(2,1)S(1)}, u32[]{:S(2)}, u32[]{:S(2)}) async-start(bf16[32,8,16,128]{3,2,1,0:T(8,128)(2,1)} %get-tuple-element.17), calls=%async_computation.1 | async-start | bytes 2097152 | tf_op jit(solution)/shard_map/all_to_all | solution.py:284
  42.8 3.4 %collective-permute-start.1 = (bf16[8,64,128]{2,1,0:T(8,128)(2,1)S(1)}, bf16[8,64,128]{2,1,0:T(8,128)(2,1)S(1)}, u32[]{:S(2)}, u32[]{:S(2)}) collective-permute-start(bf16[8,64,128]{2,1,0:T(8,128)(2,1)S(1)} %get-tuple-element.23.refs_0_), channel_id=1, source_target_pairs={{0,16},{16,32},{32,48},{48,0},{1,17},{17,33},{33,49},{49,1},{2,18}... | collective-permute-start | bytes 393224 | tf_op jit(solution)/shard_map/ppermute | solution.py:286
  46.2 4.6 %collective-permute-start.2 = (bf16[8,64,128]{2,1,0:T(8,128)(2,1)S(1)}, bf16[8,64,128]{2,1,0:T(8,128)(2,1)S(1)}, u32[]{:S(2)}, u32[]{:S(2)}) collective-permute-start(bf16[8,64,128]{2,1,0:T(8,128)(2,1)S(1)} %get-tuple-element.23.refs_0_), channel_id=1, source_target_pairs={{0,32},{16,48},{32,0},{48,16},{1,33},{17,49},{33,1},{49,17},{2,34}... | collective-permute-start | bytes 393224 | tf_op jit(solution)/shard_map/ppermute | solution.py:286
  50.7 3.4 %collective-permute-start.3 = (bf16[8,64,128]{2,1,0:T(8,128)(2,1)S(1)}, bf16[8,64,128]{2,1,0:T(8,128)(2,1)S(1)}, u32[]{:S(2)}, u32[]{:S(2)}) collective-permute-start(bf16[8,64,128]{2,1,0:T(8,128)(2,1)S(1)} %get-tuple-element.23.refs_0_), channel_id=1, source_target_pairs={{0,48},{16,0},{32,16},{48,32},{1,49},{17,1},{33,17},{49,33},{2,50}... | collective-permute-start | bytes 393224 | tf_op jit(solution)/shard_map/ppermute | solution.py:286
  54.1 0.0 collective-permute-done.par_ref
  54.1 2.0 %all-to-all-done.1 = bf16[32,8,16,128]{3,2,1,0:T(8,128)(2,1)S(1)} async-done(((bf16[32,8,16,128]{3,2,1,0:T(8,128)(2,1)}), bf16[32,8,16,128]{3,2,1,0:T(8,128)(2,1)S(1)}, u32[]{:S(2)}, u32[]{:S(2)}) %all-to-all-start.1) | async-done | bytes 1048608 | tf_op jit(solution)/shard_map/all_to_all | solution.py:284
  56.1 4.2 %shard_map.76 = f32[8,32,128]{2,1,0:T(8,128)} custom-call(bf16[4,4,2,8,16,128]{5,4,3,2,1,0:T(8,128)(2,1)S(1)} %bitcast.9, bf16[128,8192]{1,0:T(8,128)(2,1)} %bitcast.14, bf16[256,8192]{1,0:T(8,128)(2,1)} %collective-permute-done.par_ref), custom_call_target="tpu_custom_call" | custom-call | flops 268435456 | bytes 5242880 | tf_op jit(solution)/shard_map/pallas_call | solution.py:183
  60.4 0.0 collective-permute-done.1.refs_1_
  60.4 0.6 collective-permute-done.2.refs_2_
  60.9 0.0 collective-permute-done.3.refs_3_
  61.0 3.2 %collective-permute-start.5 = (bf16[4,8,64,128]{3,2,1,0:T(8,128)(2,1)S(1)}, bf16[4,8,64,128]{3,2,1,0:T(8,128)(2,1)S(1)}, u32[]{:S(2)}, u32[]{:S(2)}) collective-permute-start(bf16[4,8,64,128]{3,2,1,0:T(8,128)(2,1)S(1)} %shard_map.78.here_ref), channel_id=1, source_target_pairs={{0,1},{1,0},{2,3},{3,2},{4,5},{5,4},{6,7},{7,6},{8,9},{9,8},{10,11... | collective-permute-start | bytes 1572872 | tf_op jit(solution)/shard_map/ppermute | solution.py:292
  64.2 4.7 %all-to-all-start.2 = ((f32[8,32,128]{2,1,0:T(8,128)}), f32[8,32,128]{2,1,0:T(8,128)S(1)}, u32[]{:S(2)}, u32[]{:S(2)}) async-start(f32[8,32,128]{2,1,0:T(8,128)} %shard_map.76), calls=%async_computation.2 | async-start | bytes 262144 | tf_op jit(solution)/shard_map/all_to_all | solution.py:290
  68.9 0.0 copy-start
  68.9 4.2 %shard_map.77 = (f32[32,128]{1,0:T(8,128)S(1)}, f32[32,128]{1,0:T(8,128)}) custom-call(bf16[4,4,2,8,16,128]{5,4,3,2,1,0:T(8,128)(2,1)S(1)} %bitcast.10, bf16[128,8192]{1,0:T(8,128)(2,1)} %bitcast.16, bf16[256,8192]{1,0:T(8,128)(2,1)} %collective-permute-done.par_ref), custom_call_target="tpu_custom_call" | custom-call | flops 268435456 | bytes 5242880 | tf_op jit(solution)/shard_map/pallas_call | solution.py:195
  73.1 2.1 %collective-permute-start.4 = (f32[32,128]{1,0:T(8,128)}, f32[32,128]{1,0:T(8,128)S(1)}, u32[]{:S(2)}, u32[]{:S(2)}) collective-permute-start(f32[32,128]{1,0:T(8,128)} %get-tuple-element.22), channel_id=1, source_target_pairs={{0,64},{64,0},{1,65},{65,1},{2,66},{66,2},{3,67},{67,3},{4,68},{68... | collective-permute-start | bytes 49160 | tf_op jit(solution)/shard_map/ppermute | solution.py:294
  75.8 0.6 collective-permute-done.4.theirs_ref
  76.4 0.0 all-to-all-done.2.parts_ref
  76.4 0.0 collective-permute-done.5.there_ref
  76.4 1.7 %shard_map.79 = f32[64,128]{1,0:T(8,128)} custom-call(s32[1]{0:T(128)S(6)} %copy.9.len_ref, f32[8,32,128]{2,1,0:T(8,128)S(1)} %all-to-all-done.2.parts_ref, f32[32,128]{1,0:T(8,128)S(1)} %get-tuple-element.21.mine_ref, f32[32,128]{1,0:T(8,128)S(1)} %collective-permute-done.4.theirs_ref, bf16[4,8,64,128]{3,2,1,0:T(8,128)(2,1)S(1)} %shard_map.78.here_ref, ...), custom_call_target="tpu_custom_call" | custom-call | flops 1048576 | bytes 1048576 | tf_op jit(solution)/shard_map/pallas_call | solution.py:247
  78.1 21.7 %all_to_all.20 = f32[64,1,128]{2,1,0:T(1,128)S(1)} all-to-all(f32[64,1,128]{2,1,0:T(1,128)} %bitcast.17), channel_id=1, replica_groups=mesh['x'=4,'c'=2,'y'=4,'u'=8,'p'=2] {'y','u','p'}, dimensions={0} | all-to-all | bytes 65536 | tf_op jit(solution)/shard_map/all_to_all | solution.py:296
  99.9 0.0 copy-done
  99.9 0.9 shard_map.80
  (1 shorter events, 0.0 us)
Async XLA Ops:
  1.5 32.4 %all-to-all-start = ((bf16[8,80,128]{2,1,0:T(8,128)(2,1)}), bf16[8,80,128]{2,1,0:T(8,128)(2,1)S(1)}, u32[]{:S(2)}, u32[]{:S(2)}) async-start(bf16[8,80,128]{2,1,0:T(8,128)(2,1)} %shard_map.73), calls=%async_computation | async-start | bytes 327680 | tf_op jit(solution)/shard_map/all_to_all | solution.py:280
  19.9 34.3 %collective-permute-start = (bf16[256,8192]{1,0:T(8,128)(2,1)}, bf16[256,8192]{1,0:T(8,128)(2,1)}, u32[]{:S(2)}, u32[]{:S(2)}) collective-permute-start(bf16[256,8192]{1,0:T(8,128)(2,1)} %get-tuple-element.18), channel_id=1, source_target_pairs={{0,64},{64,0},{1,65},{65,1},{2,66},{66,2},{3,67},{67,3},{4,68},{68... | collective-permute-start | bytes 12582920 | tf_op jit(solution)/shard_map/ppermute | solution.py:282
  35.1 21.0 %all-to-all-start.1 = ((bf16[32,8,16,128]{3,2,1,0:T(8,128)(2,1)}), bf16[32,8,16,128]{3,2,1,0:T(8,128)(2,1)S(1)}, u32[]{:S(2)}, u32[]{:S(2)}) async-start(bf16[32,8,16,128]{3,2,1,0:T(8,128)(2,1)} %get-tuple-element.17), calls=%async_computation.1 | async-start | bytes 2097152 | tf_op jit(solution)/shard_map/all_to_all | solution.py:284
  42.8 17.6 %collective-permute-start.1 = (bf16[8,64,128]{2,1,0:T(8,128)(2,1)S(1)}, bf16[8,64,128]{2,1,0:T(8,128)(2,1)S(1)}, u32[]{:S(2)}, u32[]{:S(2)}) collective-permute-start(bf16[8,64,128]{2,1,0:T(8,128)(2,1)S(1)} %get-tuple-element.23.refs_0_), channel_id=1, source_target_pairs={{0,16},{16,32},{32,48},{48,0},{1,17},{17,33},{33,49},{49,1},{2,18}... | collective-permute-start | bytes 393224 | tf_op jit(solution)/shard_map/ppermute | solution.py:286
  46.2 14.8 %collective-permute-start.2 = (bf16[8,64,128]{2,1,0:T(8,128)(2,1)S(1)}, bf16[8,64,128]{2,1,0:T(8,128)(2,1)S(1)}, u32[]{:S(2)}, u32[]{:S(2)}) collective-permute-start(bf16[8,64,128]{2,1,0:T(8,128)(2,1)S(1)} %get-tuple-element.23.refs_0_), channel_id=1, source_target_pairs={{0,32},{16,48},{32,0},{48,16},{1,33},{17,49},{33,1},{49,17},{2,34}... | collective-permute-start | bytes 393224 | tf_op jit(solution)/shard_map/ppermute | solution.py:286
  50.7 10.2 %collective-permute-start.3 = (bf16[8,64,128]{2,1,0:T(8,128)(2,1)S(1)}, bf16[8,64,128]{2,1,0:T(8,128)(2,1)S(1)}, u32[]{:S(2)}, u32[]{:S(2)}) collective-permute-start(bf16[8,64,128]{2,1,0:T(8,128)(2,1)S(1)} %get-tuple-element.23.refs_0_), channel_id=1, source_target_pairs={{0,48},{16,0},{32,16},{48,32},{1,49},{17,1},{33,17},{49,33},{2,50}... | collective-permute-start | bytes 393224 | tf_op jit(solution)/shard_map/ppermute | solution.py:286
  61.0 15.4 %collective-permute-start.5 = (bf16[4,8,64,128]{3,2,1,0:T(8,128)(2,1)S(1)}, bf16[4,8,64,128]{3,2,1,0:T(8,128)(2,1)S(1)}, u32[]{:S(2)}, u32[]{:S(2)}) collective-permute-start(bf16[4,8,64,128]{3,2,1,0:T(8,128)(2,1)S(1)} %shard_map.78.here_ref), channel_id=1, source_target_pairs={{0,1},{1,0},{2,3},{3,2},{4,5},{5,4},{6,7},{7,6},{8,9},{9,8},{10,11... | collective-permute-start | bytes 1572872 | tf_op jit(solution)/shard_map/ppermute | solution.py:292
  64.2 12.2 %all-to-all-start.2 = ((f32[8,32,128]{2,1,0:T(8,128)}), f32[8,32,128]{2,1,0:T(8,128)S(1)}, u32[]{:S(2)}, u32[]{:S(2)}) async-start(f32[8,32,128]{2,1,0:T(8,128)} %shard_map.76), calls=%async_computation.2 | async-start | bytes 262144 | tf_op jit(solution)/shard_map/all_to_all | solution.py:290
  68.9 31.0 %copy-start = (s32[64]{0:T(128)S(1)}, s32[64]{0:T(128)}, u32[]{:S(2)}) copy-start(s32[64]{0:T(128)} %param.13) | copy-start | bytes 772
  73.1 3.3 %collective-permute-start.4 = (f32[32,128]{1,0:T(8,128)}, f32[32,128]{1,0:T(8,128)S(1)}, u32[]{:S(2)}, u32[]{:S(2)}) collective-permute-start(f32[32,128]{1,0:T(8,128)} %get-tuple-element.22), channel_id=1, source_target_pairs={{0,64},{64,0},{1,65},{65,1},{2,66},{66,2},{3,67},{67,3},{4,68},{68... | collective-permute-start | bytes 49160 | tf_op jit(solution)/shard_map/ppermute | solution.py:294

commit v6 on v5

--- a/solution.py
+++ b/solution.py
@@ -54,7 +54,7 @@
     )(*in_hbm(proj_in, proj_out, valid_rows))
 
 
-def stack_kernel(inc_ref, act_ref, both_ref, done_ref, data_ref, in_sems, out_sems):
+def stack_kernel(inc_ref, act_ref, both_ref, order_ref, data_ref, in_sems, out_sems):
     arrive, leave = [], []
     for j, ref in enumerate((inc_ref, act_ref)):
         for k in range(2):
@@ -67,7 +67,13 @@
             )
     for copy in arrive:
         copy.start()
-    done_ref[...] = jnp.zeros_like(done_ref)
+    my_y, my_p = lax.axis_index("y"), lax.axis_index("p")
+    came = lax.broadcasted_iota(jnp.int32, (128, 128), 0)
+    y = (my_y + 4 - ((came >> 4) & 3)) & 3
+    p = (my_p + (came >> 6)) & 1
+    goes = y * 32 + ((came >> 1) & 7) * 4 + p * 2 + (came & 1)
+    order = jnp.where(goes == lax.broadcasted_iota(jnp.int32, (128, 128), 1), 1.0, 0.0)
+    order_ref[...] = order.astype(f32)
     for first, second in zip(arrive, leave):
         first.wait()
         second.start()
@@ -78,7 +84,7 @@
 def stack(inc, act):
     return pl.pallas_call(
         stack_kernel,
-        out_shape=(pltpu.HBM((256, 8192), bf16), jax.ShapeDtypeStruct((8, 128), f32)),
+        out_shape=(pltpu.HBM((256, 8192), bf16), jax.ShapeDtypeStruct((128, 128), f32)),
         in_specs=[HBM, HBM],
         out_specs=(HBM, VMEM),
         scratch_shapes=[
@@ -91,12 +97,12 @@
     )(*in_hbm(inc, act))
 
 
-def split_kernel(got_ref, stacked_ref, proj_ref, valid_ref):
+def split_kernel(got_ref, order_ref, proj_ref, valid_ref):
     proj_ref[...] = jnp.broadcast_to(got_ref[:, 0:16][None], (NX * NY * NP, NU, 16, 128))
     valid_ref[...] = got_ref[:, 16:80]
 
 
-def split(got, stacked):
+def split(got, order):
     return pl.pallas_call(
         split_kernel,
         out_shape=(
@@ -107,7 +113,7 @@
         out_specs=(VMEM, VMEM),
         compiler_params=params(32),
         cost_estimate=cost(0, 1536 * 1024),
-    )(got, stacked)
+    )(got, order)
 
 
 def merge_kernel(*refs):
@@ -143,7 +149,7 @@
     for half in range(2):
         w = jnp.concatenate(
             [
-                w_ref[:, y, p, u].reshape(NX * 16, 128)
+                w_ref[p, :, y, u].reshape(NX * 16, 128)
                 for y in range(2 * half, 2 * half + 2)
                 for u in range(NU)
                 for p in range(NP)
@@ -203,8 +209,8 @@
     )(w, *in_hbm(own, par))
 
 
-def score_kernel(len_ref, parts_ref, mine_ref, theirs_ref, here_ref, there_ref, out_ref):
-    my_c, my_y, my_p = lax.axis_index("c"), lax.axis_index("y"), lax.axis_index("p")
+def score_kernel(len_ref, order_ref, parts_ref, mine_ref, theirs_ref, here_ref, there_ref, out_ref):
+    my_c = lax.axis_index("c")
     live = len_ref[0]
     tok = lax.broadcasted_iota(jnp.int32, (32, 128), 1)
     weight = jnp.where(tok < live, 1.0, 0.0).astype(f32) / live.astype(f32)
@@ -230,28 +236,22 @@
         ],
         axis=0,
     )
-    came = lax.broadcasted_iota(jnp.int32, (128, 128), 0)
-    y = (my_y + 4 - ((came >> 4) & 3)) & 3
-    p = (my_p + (came >> 6)) & 1
-    goes = y * 32 + ((came >> 1) & 7) * 4 + p * 2 + (came & 1)
-    order = jnp.where(goes == lax.broadcasted_iota(jnp.int32, (128, 128), 1), 1.0, 0.0)
     scores = lax.dot_general(
-        jnp.ones((64, 128), f32), part, NT, precision=HIGHEST, preferred_element_type=f32
-    )
-    out_ref[...] = jnp.dot(
-        scores, order.astype(f32), precision=HIGHEST, preferred_element_type=f32
-    )
-
-
-def score(lengths, parts, mine, theirs, here, there):
+        jnp.ones((8, 128), f32), part, NT, precision=HIGHEST, preferred_element_type=f32
+    )
+    scores = jnp.dot(scores, order_ref[...], precision=HIGHEST, preferred_element_type=f32)
+    out_ref[...] = jnp.concatenate([scores] * 8, axis=0)
+
+
+def score(lengths, order, parts, mine, theirs, here, there):
     return pl.pallas_call(
         score_kernel,
         out_shape=pltpu.HBM((64, 128), f32),
-        in_specs=[SMEM] + [VMEM] * 5,
+        in_specs=[SMEM] + [VMEM] * 6,
         out_specs=VMEM,
         compiler_params=params(32),
         cost_estimate=cost(2 * 128 * 4096, MIB),
-    )(lengths, parts, mine, theirs, here, there)
+    )(lengths, order, parts, mine, theirs, here, there)
 
 
 def gram_kernel(dom_ref, scores_ref, out_ref):
@@ -278,10 +278,10 @@
     swap = [(0, 1), (1, 0)]
     act_own, inc_own = acts[0], incoming[0]
     got = lax.all_to_all(pack(proj_in, proj_out, valid_rows), "u", 0, 0)
-    both, stacked = stack(inc_own, act_own)
+    both, order = stack(inc_own, act_own)
     par = lax.ppermute(both, "c", swap)
-    sent, valid = split(got, stacked)
-    w = lax.all_to_all(sent, ("x", "y", "p"), 0, 0).reshape(NX, NY, NP, NU, 16, 128)
+    sent, valid = split(got, order)
+    w = lax.all_to_all(sent, ("p", "x", "y"), 0, 0).reshape(NP, NX, NY, NU, 16, 128)
     came = [valid] + [
         lax.ppermute(valid, "y", [(i, (i + k) % NY) for i in range(NY)]) for k in range(1, NY)
     ]
@@ -292,7 +292,7 @@
     there = lax.ppermute(here, "p", swap)
     mine, others = project_acts(w, act_own, par)
     theirs = lax.ppermute(others, "c", swap)
-    scores = score(lengths, parts, mine, theirs, here, there)
+    scores = score(lengths, order, parts, mine, theirs, here, there)
     scores = lax.all_to_all(scores.reshape(64, 1, 128), ("y", "u", "p"), 0, 0).reshape(64, 128)
     return gram(domains.reshape(1, 64), scores)[None, None]
 

time: 101 us -> 101 us (level)
  transfers between devices with their start and end apart: 9 -> 9, of which waited for: 4 -> 5; matrix products, arithmetic and copies ran while one was open for 0% -> 0% of each run, Pallas kernels for 13% -> 13%
where the time goes in v6:
time: 101 us
  starting transfers between devices  45.5 us (45%)
  blocking collectives  21.8 us (22%)
  Pallas kernels  17.1 us (17%)
  waiting for transfers between devices  15.6 us (15%)
    all_to_all x1, blocking collectives, body(): lax.all_to_all(scores.reshape(64, 1, 128), ('y', 'u', 'p'), 0, 0)  21.8 us
    all_to_all x1, starting transfers between devices, body(): got = lax.all_to_all(pack(proj_in, proj_out, valid_rows), 'u', 0, 0)  15.1 us
    all_to_all x1, waiting for transfers between devices, body(): got = lax.all_to_all(pack(proj_in, proj_out, valid_rows), 'u', 0, 0)  12 us
    ppermute x3, starting transfers between devices, body(): lax.ppermute(valid, 'y', [(i, (i + k) % NY) for i in range(NY)])  11.3 us
    all_to_all x1, starting transfers between devices, body(): lax.all_to_all(sent, ('p', 'x', 'y'), 0, 0).reshape(NP, NX, NY, NU, 16, 128)  7.62 us
    all_to_all x1, starting transfers between devices, body(): parts = lax.all_to_all(sums, ('x', 'c'), 0, 0)  4.53 us
    pallas_call x1, Pallas kernels, project_grads(): pl.pallas_call(grad_kernel, out_shape=pltpu.HBM((NX * NC, 32, 128), f32),...  4.24 us
    pallas_call x1, Pallas kernels, project_acts(): pl.pallas_call(act_kernel, out_shape=(jax.ShapeDtypeStruct((32, 128), f32...  4.2 us
  transfers between devices with their start and end apart: 9, of which 5 were waited for; matrix products, arithmetic and copies ran while one was open for 0% of the time, Pallas kernels for 13%

profile of v6, /device:TPU:2, one launch (start us, length us, event | category | flops | bytes accessed | tf_op | source)
XLA Modules:
  0.0 100.7 jit_solution(4155394499749842803)
XLA Ops:
  0.0 1.5 %shard_map.74 = bf16[8,80,128]{2,1,0:T(8,128)(2,1)} custom-call(bf16[64,128]{1,0:T(8,128)(2,1)} %in_ref.1, bf16[64,128]{1,0:T(8,128)(2,1)} %out_ref.1, bf16[1,2,4096]{2,1,0:T(2,128)(2,1)} %valid_ref.1), custom_call_target="tpu_custom_call" | custom-call | bytes 212992 | tf_op jit(solution)/shard_map/pallas_call | solution.py:46
  1.5 15.1 %all-to-all-start = ((bf16[8,80,128]{2,1,0:T(8,128)(2,1)}), bf16[8,80,128]{2,1,0:T(8,128)(2,1)S(1)}, u32[]{:S(2)}, u32[]{:S(2)}) async-start(bf16[8,80,128]{2,1,0:T(8,128)(2,1)} %shard_map.74), calls=%async_computation | async-start | bytes 327680 | tf_op jit(solution)/shard_map/all_to_all | solution.py:280
  16.5 3.3 %shard_map.73 = (bf16[256,8192]{1,0:T(8,128)(2,1)}, f32[128,128]{1,0:T(8,128)S(1)}) custom-call(bf16[128,8192]{1,0:T(8,128)(2,1)} %bitcast.13, bf16[128,8192]{1,0:T(8,128)(2,1)} %bitcast.15), custom_call_target="tpu_custom_call" | custom-call | bytes 8388608 | tf_op jit(solution)/shard_map/pallas_call | solution.py:85
  19.9 1.9 %collective-permute-start = (bf16[256,8192]{1,0:T(8,128)(2,1)}, bf16[256,8192]{1,0:T(8,128)(2,1)}, u32[]{:S(2)}, u32[]{:S(2)}) collective-permute-start(bf16[256,8192]{1,0:T(8,128)(2,1)} %get-tuple-element.18), channel_id=1, source_target_pairs={{0,64},{64,0},{1,65},{65,1},{2,66},{66,2},{3,67},{67,3},{4,68},{68... | collective-permute-start | bytes 12582920 | tf_op jit(solution)/shard_map/ppermute | solution.py:282
  21.8 12.0 %all-to-all-done.got_ref = bf16[8,80,128]{2,1,0:T(8,128)(2,1)S(1)} async-done(((bf16[8,80,128]{2,1,0:T(8,128)(2,1)}), bf16[8,80,128]{2,1,0:T(8,128)(2,1)S(1)}, u32[]{:S(2)}, u32[]{:S(2)}) %all-to-all-start) | async-done | bytes 163872 | tf_op jit(solution)/shard_map/all_to_all | solution.py:280
  33.8 1.3 %shard_map.75 = (bf16[32,8,16,128]{3,2,1,0:T(8,128)(2,1)}, bf16[8,64,128]{2,1,0:T(8,128)(2,1)S(1)}) custom-call(bf16[8,80,128]{2,1,0:T(8,128)(2,1)S(1)} %all-to-all-done.got_ref, f32[128,128]{1,0:T(8,128)S(1)} %get-tuple-element.16.order_ref), custom_call_target="tpu_custom_call" | custom-call | bytes 1572864 | tf_op jit(solution)/shard_map/pallas_call | solution.py:106
  35.1 7.6 %all-to-all-start.1 = ((bf16[32,8,16,128]{3,2,1,0:T(8,128)(2,1)}), bf16[32,8,16,128]{3,2,1,0:T(8,128)(2,1)S(1)}, u32[]{:S(2)}, u32[]{:S(2)}) async-start(bf16[32,8,16,128]{3,2,1,0:T(8,128)(2,1)} %get-tuple-element.17), calls=%async_computation.1 | async-start | bytes 2097152 | tf_op jit(solution)/shard_map/all_to_all | solution.py:284
  42.8 3.4 %collective-permute-start.1 = (bf16[8,64,128]{2,1,0:T(8,128)(2,1)S(1)}, bf16[8,64,128]{2,1,0:T(8,128)(2,1)S(1)}, u32[]{:S(2)}, u32[]{:S(2)}) collective-permute-start(bf16[8,64,128]{2,1,0:T(8,128)(2,1)S(1)} %get-tuple-element.23.refs_0_), channel_id=1, source_target_pairs={{0,16},{16,32},{32,48},{48,0},{1,17},{17,33},{33,49},{49,1},{2,18}... | collective-permute-start | bytes 393224 | tf_op jit(solution)/shard_map/ppermute | solution.py:286
  46.1 4.6 %collective-permute-start.2 = (bf16[8,64,128]{2,1,0:T(8,128)(2,1)S(1)}, bf16[8,64,128]{2,1,0:T(8,128)(2,1)S(1)}, u32[]{:S(2)}, u32[]{:S(2)}) collective-permute-start(bf16[8,64,128]{2,1,0:T(8,128)(2,1)S(1)} %get-tuple-element.23.refs_0_), channel_id=1, source_target_pairs={{0,32},{16,48},{32,0},{48,16},{1,33},{17,49},{33,1},{49,17},{2,34}... | collective-permute-start | bytes 393224 | tf_op jit(solution)/shard_map/ppermute | solution.py:286
  50.7 3.4 %collective-permute-start.3 = (bf16[8,64,128]{2,1,0:T(8,128)(2,1)S(1)}, bf16[8,64,128]{2,1,0:T(8,128)(2,1)S(1)}, u32[]{:S(2)}, u32[]{:S(2)}) collective-permute-start(bf16[8,64,128]{2,1,0:T(8,128)(2,1)S(1)} %get-tuple-element.23.refs_0_), channel_id=1, source_target_pairs={{0,48},{16,0},{32,16},{48,32},{1,49},{17,1},{33,17},{49,33},{2,50}... | collective-permute-start | bytes 393224 | tf_op jit(solution)/shard_map/ppermute | solution.py:286
  54.1 0.0 collective-permute-done.par_ref
  54.1 2.4 %all-to-all-done.1 = bf16[32,8,16,128]{3,2,1,0:T(8,128)(2,1)S(1)} async-done(((bf16[32,8,16,128]{3,2,1,0:T(8,128)(2,1)}), bf16[32,8,16,128]{3,2,1,0:T(8,128)(2,1)S(1)}, u32[]{:S(2)}, u32[]{:S(2)}) %all-to-all-start.1) | async-done | bytes 1048608 | tf_op jit(solution)/shard_map/all_to_all | solution.py:284
  56.5 4.2 %shard_map.76 = f32[8,32,128]{2,1,0:T(8,128)} custom-call(bf16[2,4,4,8,16,128]{5,4,3,2,1,0:T(8,128)(2,1)S(1)} %bitcast.9, bf16[128,8192]{1,0:T(8,128)(2,1)} %bitcast.14, bf16[256,8192]{1,0:T(8,128)(2,1)} %collective-permute-done.par_ref), custom_call_target="tpu_custom_call" | custom-call | flops 268435456 | bytes 5242880 | tf_op jit(solution)/shard_map/pallas_call | solution.py:189
  60.7 0.0 collective-permute-done.1.refs_1_
  60.7 0.6 collective-permute-done.2.refs_2_
  61.3 0.0 collective-permute-done.3.refs_3_
  61.3 2.9 %collective-permute-start.5 = (bf16[4,8,64,128]{3,2,1,0:T(8,128)(2,1)S(1)}, bf16[4,8,64,128]{3,2,1,0:T(8,128)(2,1)S(1)}, u32[]{:S(2)}, u32[]{:S(2)}) collective-permute-start(bf16[4,8,64,128]{3,2,1,0:T(8,128)(2,1)S(1)} %shard_map.78.here_ref), channel_id=1, source_target_pairs={{0,1},{1,0},{2,3},{3,2},{4,5},{5,4},{6,7},{7,6},{8,9},{9,8},{10,11... | collective-permute-start | bytes 1572872 | tf_op jit(solution)/shard_map/ppermute | solution.py:292
  64.3 4.5 %all-to-all-start.2 = ((f32[8,32,128]{2,1,0:T(8,128)}), f32[8,32,128]{2,1,0:T(8,128)S(1)}, u32[]{:S(2)}, u32[]{:S(2)}) async-start(f32[8,32,128]{2,1,0:T(8,128)} %shard_map.76), calls=%async_computation.2 | async-start | bytes 262144 | tf_op jit(solution)/shard_map/all_to_all | solution.py:290
  68.8 0.0 copy-start
  68.8 4.2 %shard_map.77 = (f32[32,128]{1,0:T(8,128)S(1)}, f32[32,128]{1,0:T(8,128)}) custom-call(bf16[2,4,4,8,16,128]{5,4,3,2,1,0:T(8,128)(2,1)S(1)} %bitcast.10, bf16[128,8192]{1,0:T(8,128)(2,1)} %bitcast.16, bf16[256,8192]{1,0:T(8,128)(2,1)} %collective-permute-done.par_ref), custom_call_target="tpu_custom_call" | custom-call | flops 268435456 | bytes 5242880 | tf_op jit(solution)/shard_map/pallas_call | solution.py:201
  73.0 2.1 %collective-permute-start.4 = (f32[32,128]{1,0:T(8,128)}, f32[32,128]{1,0:T(8,128)S(1)}, u32[]{:S(2)}, u32[]{:S(2)}) collective-permute-start(f32[32,128]{1,0:T(8,128)} %get-tuple-element.22), channel_id=1, source_target_pairs={{0,64},{64,0},{1,65},{65,1},{2,66},{66,2},{3,67},{67,3},{4,68},{68... | collective-permute-start | bytes 49160 | tf_op jit(solution)/shard_map/ppermute | solution.py:294
  75.7 0.6 collective-permute-done.4.theirs_ref
  76.3 0.0 all-to-all-done.2.parts_ref
  76.3 0.1 collective-permute-done.5.there_ref
  76.4 1.7 %shard_map.79 = f32[64,128]{1,0:T(8,128)} custom-call(s32[1]{0:T(128)S(6)} %copy.9.len_ref, f32[128,128]{1,0:T(8,128)S(1)} %get-tuple-element.16.order_ref, f32[8,32,128]{2,1,0:T(8,128)S(1)} %all-to-all-done.2.parts_ref, f32[32,128]{1,0:T(8,128)S(1)} %get-tuple-element.21.mine_ref, f32[32,128]{1,0:T(8,128)S(1)} %collective-permute-done.4.theirs_ref, ...), custom_call_target="tpu_custom_call" | custom-call | flops 1048576 | bytes 1048576 | tf_op jit(solution)/shard_map/pallas_call | solution.py:247
  78.1 21.8 %all_to_all.20 = f32[64,1,128]{2,1,0:T(1,128)S(1)} all-to-all(f32[64,1,128]{2,1,0:T(1,128)} %bitcast.17), channel_id=1, replica_groups=mesh['x'=4,'c'=2,'y'=4,'u'=8,'p'=2] {'y','u','p'}, dimensions={0} | all-to-all | bytes 65536 | tf_op jit(solution)/shard_map/all_to_all | solution.py:296
  99.8 0.0 copy-done
  99.8 0.9 shard_map.80
  (1 shorter events, 0.0 us)
Async XLA Ops:
  1.5 32.4 %all-to-all-start = ((bf16[8,80,128]{2,1,0:T(8,128)(2,1)}), bf16[8,80,128]{2,1,0:T(8,128)(2,1)S(1)}, u32[]{:S(2)}, u32[]{:S(2)}) async-start(bf16[8,80,128]{2,1,0:T(8,128)(2,1)} %shard_map.74), calls=%async_computation | async-start | bytes 327680 | tf_op jit(solution)/shard_map/all_to_all | solution.py:280
  19.9 34.3 %collective-permute-start = (bf16[256,8192]{1,0:T(8,128)(2,1)}, bf16[256,8192]{1,0:T(8,128)(2,1)}, u32[]{:S(2)}, u32[]{:S(2)}) collective-permute-start(bf16[256,8192]{1,0:T(8,128)(2,1)} %get-tuple-element.18), channel_id=1, source_target_pairs={{0,64},{64,0},{1,65},{65,1},{2,66},{66,2},{3,67},{67,3},{4,68},{68... | collective-permute-start | bytes 12582920 | tf_op jit(solution)/shard_map/ppermute | solution.py:282
  35.1 21.3 %all-to-all-start.1 = ((bf16[32,8,16,128]{3,2,1,0:T(8,128)(2,1)}), bf16[32,8,16,128]{3,2,1,0:T(8,128)(2,1)S(1)}, u32[]{:S(2)}, u32[]{:S(2)}) async-start(bf16[32,8,16,128]{3,2,1,0:T(8,128)(2,1)} %get-tuple-element.17), calls=%async_computation.1 | async-start | bytes 2097152 | tf_op jit(solution)/shard_map/all_to_all | solution.py:284
  42.8 18.0 %collective-permute-start.1 = (bf16[8,64,128]{2,1,0:T(8,128)(2,1)S(1)}, bf16[8,64,128]{2,1,0:T(8,128)(2,1)S(1)}, u32[]{:S(2)}, u32[]{:S(2)}) collective-permute-start(bf16[8,64,128]{2,1,0:T(8,128)(2,1)S(1)} %get-tuple-element.23.refs_0_), channel_id=1, source_target_pairs={{0,16},{16,32},{32,48},{48,0},{1,17},{17,33},{33,49},{49,1},{2,18}... | collective-permute-start | bytes 393224 | tf_op jit(solution)/shard_map/ppermute | solution.py:286
  46.1 15.2 %collective-permute-start.2 = (bf16[8,64,128]{2,1,0:T(8,128)(2,1)S(1)}, bf16[8,64,128]{2,1,0:T(8,128)(2,1)S(1)}, u32[]{:S(2)}, u32[]{:S(2)}) collective-permute-start(bf16[8,64,128]{2,1,0:T(8,128)(2,1)S(1)} %get-tuple-element.23.refs_0_), channel_id=1, source_target_pairs={{0,32},{16,48},{32,0},{48,16},{1,33},{17,49},{33,1},{49,17},{2,34}... | collective-permute-start | bytes 393224 | tf_op jit(solution)/shard_map/ppermute | solution.py:286
  50.7 10.6 %collective-permute-start.3 = (bf16[8,64,128]{2,1,0:T(8,128)(2,1)S(1)}, bf16[8,64,128]{2,1,0:T(8,128)(2,1)S(1)}, u32[]{:S(2)}, u32[]{:S(2)}) collective-permute-start(bf16[8,64,128]{2,1,0:T(8,128)(2,1)S(1)} %get-tuple-element.23.refs_0_), channel_id=1, source_target_pairs={{0,48},{16,0},{32,16},{48,32},{1,49},{17,1},{33,17},{49,33},{2,50}... | collective-permute-start | bytes 393224 | tf_op jit(solution)/shard_map/ppermute | solution.py:286
  61.3 15.0 %collective-permute-start.5 = (bf16[4,8,64,128]{3,2,1,0:T(8,128)(2,1)S(1)}, bf16[4,8,64,128]{3,2,1,0:T(8,128)(2,1)S(1)}, u32[]{:S(2)}, u32[]{:S(2)}) collective-permute-start(bf16[4,8,64,128]{3,2,1,0:T(8,128)(2,1)S(1)} %shard_map.78.here_ref), channel_id=1, source_target_pairs={{0,1},{1,0},{2,3},{3,2},{4,5},{5,4},{6,7},{7,6},{8,9},{9,8},{10,11... | collective-permute-start | bytes 1572872 | tf_op jit(solution)/shard_map/ppermute | solution.py:292
  64.3 12.0 %all-to-all-start.2 = ((f32[8,32,128]{2,1,0:T(8,128)}), f32[8,32,128]{2,1,0:T(8,128)S(1)}, u32[]{:S(2)}, u32[]{:S(2)}) async-start(f32[8,32,128]{2,1,0:T(8,128)} %shard_map.76), calls=%async_computation.2 | async-start | bytes 262144 | tf_op jit(solution)/shard_map/all_to_all | solution.py:290
  68.8 31.1 %copy-start = (s32[64]{0:T(128)S(1)}, s32[64]{0:T(128)}, u32[]{:S(2)}) copy-start(s32[64]{0:T(128)} %param.13) | copy-start | bytes 772
  73.0 3.3 %collective-permute-start.4 = (f32[32,128]{1,0:T(8,128)}, f32[32,128]{1,0:T(8,128)S(1)}, u32[]{:S(2)}, u32[]{:S(2)}) collective-permute-start(f32[32,128]{1,0:T(8,128)} %get-tuple-element.22), channel_id=1, source_target_pairs={{0,64},{64,0},{1,65},{65,1},{2,66},{66,2},{3,67},{67,3},{4,68},{68... | collective-permute-start | bytes 49160 | tf_op jit(solution)/shard_map/ppermute | solution.py:294
